TPU v7x, 256 devices: a whole 4x4x8 slice. The times are simulated.
256 devices in a mesh: bead: 16 (over x_hi, z), space: 16 (over x_lo, y, core).
Axes of the slice: x: 4 (x_hi: 2, x_lo: 2; x = x_hi * 2 + x_lo), y: 4, z: 8, core: 2. Of those that a mesh axis runs over, the one named last changes fastest.
Arguments:
- coords: float32 [32, 3, 4096], P('bead', None, 'space'), may hold values from -6 to 6
- momenta: float32 [32, 3, 4096], P('bead', None, 'space'), may hold values from -12 to 12
- species: int32 [4096], P('space'), may hold values from 0 to 4
- atom_features: float32 [4096, 128], P('space'), may hold values from -4 to 4
- neighbours: int32 [32, 4096, 16], P('bead', 'space'), may hold values from -1 to 511, as said below
- ghost_rows: int32 [32, 4096], P('bead', 'space'), may hold values from 0 to 255
- embed: float32 [5, 128], replicated, may hold values from -5 to 5
- w_filter: float32 [2, 16, 128], replicated, may hold values from -1.5 to 1.5
- w_value: bfloat16 [2, 128, 128], replicated, may hold values from -0.5 to 0.5
- w_out: bfloat16 [2, 128, 128], replicated, may hold values from -0.5 to 0.5
- readout: float32 [128], replicated, may hold values from -0.5 to 0.5
Outputs:
- new_coords: float32 [32, 3, 4096], P('bead', None, 'space')
- new_momenta: float32 [32, 3, 4096], P('bead', None, 'space')
Inputs may be any that keep to these rules, and one draw needn't show every extreme that they name: `neighbours`: each entry is -1 (empty slot) or an index into the domain's extended numbering: 256 own atoms, then 128 atoms from the domain on the left, then 128 from the domain on the right. `ghost_rows`: entries are own-atom indices of the domain; in a domain's block of 256, the first half goes to the domain on its left, the second half to the one on its right; the domains form a closed cycle.
All inputs are finite; a program needn't handle non-finite values.
Results may differ from a plain program's by a relative error of at most 0.015.
Values may be sent and summed in bfloat16 or wider, within the bound.
A program may use at most 64 MiB of HBM per device.

v0:
```python
import math

import jax
import jax.numpy as jnp
from jax import lax
from jax.sharding import PartitionSpec as P

MASSES = (1.008, 12.011, 14.007, 15.999, 30.974)
STEP_DT = 1.0
OMEGA_P = 0.6
WIDTH = 3.125
SPACING = 0.25
SOFTEN = 0.01


def padded(value, sides, width):
    for axis, dim in sides:
        size, length = (lax.axis_size(axis), value.shape[dim])
        up = [(i, (i + 1) % size) for i in range(size)]
        down = [(j, i) for i, j in up]
        last = lax.slice_in_dim(value, length - width, length, axis=dim)
        initial = lax.slice_in_dim(value, 0, width, axis=dim)
        before = lax.ppermute(last, axis, up)
        after = lax.ppermute(initial, axis, down)
        value = jnp.concatenate([before, value, after], axis=dim)
    return value


def value_rows(hidden, weight):
    shape = hidden.shape
    flat = hidden.astype(jnp.bfloat16).reshape(-1, shape[-1])
    return jnp.dot(flat, weight, preferred_element_type=jnp.float32).reshape(
        shape[:-1] + (weight.shape[1],)
    )


def mix_layer(hidden, message, weight):
    shape = message.shape
    flat = message.astype(jnp.bfloat16).reshape(-1, shape[-1])
    update = jnp.dot(flat, weight, preferred_element_type=jnp.float32).reshape(shape)
    return hidden + jax.nn.silu(update)


def selection_table(lists, extent):
    bead_count, own_count, slots = lists.shape
    flat = lists.reshape(bead_count, own_count * slots)
    columns = jnp.arange(extent, dtype=jnp.int32)
    return (flat[:, :, None] == columns[None, None, :]).astype(jnp.float32)


def edge_messages(values, positions, lists, selector, w_radial):
    bead_count, own_count, slots = lists.shape
    present = (lists >= 0).astype(jnp.float32)
    own_xyz = positions[:, :, :own_count]
    far_xyz = jnp.einsum("bej,bcj->bce", selector, positions, precision=lax.Precision.HIGHEST)
    far_xyz = far_xyz.reshape(bead_count, 3, own_count, slots)
    offset = far_xyz - own_xyz[:, :, :, None]
    distance = jnp.sqrt(jnp.sum(offset * offset, axis=1) + SOFTEN)
    centers = SPACING * jnp.arange(w_radial.shape[0], dtype=jnp.float32)
    radial = jnp.exp(-WIDTH * (distance[..., None] - centers) ** 2)
    filters = jnp.einsum("bakn,nc->bakc", radial, w_radial, precision=lax.Precision.HIGHEST)
    far_values = jnp.einsum("bej,bjc->bec", selector, values, precision=lax.Precision.HIGHEST)
    far_values = far_values.reshape(bead_count, own_count, slots, values.shape[2])
    return jnp.sum(filters * far_values * present[..., None], axis=2)


def normal_table(count):
    j_index = jnp.arange(count, dtype=jnp.float32)[:, None]
    k_index = jnp.arange(count, dtype=jnp.float32)[None, :]
    angle = 2.0 * math.pi * j_index * k_index / count
    border = (k_index == 0.0) | (k_index == float(count // 2))
    inner = jnp.where(k_index < count / 2.0, jnp.cos(angle), jnp.sin(angle)) * math.sqrt(
        2.0 / count
    )
    matrix = jnp.where(border, jnp.cos(angle) / math.sqrt(count), inner)
    omegas = 2.0 * OMEGA_P * jnp.sin(math.pi * jnp.arange(count, dtype=jnp.float32) / count)
    return (matrix, omegas)


def advance(normal_modes, omegas, masses):
    positions_m = normal_modes[:, :3]
    momenta_m = normal_modes[:, 3:]
    freq = omegas[:, None, None]
    guarded = jnp.where(freq > 0.0, freq, 1.0)
    cosine = jnp.cos(freq * STEP_DT)
    sine_term = jnp.sin(freq * STEP_DT)
    drift_term = jnp.where(freq > 0.0, sine_term / guarded, STEP_DT)
    new_positions = cosine * positions_m + drift_term * momenta_m / masses
    new_momenta = cosine * momenta_m - masses * freq * sine_term * positions_m
    return jnp.concatenate([new_positions, new_momenta], axis=1)


def local(
    coords,
    momenta,
    species,
    atom_features,
    neighbours,
    ghost_rows,
    embed,
    w_filter,
    w_value,
    w_out,
    readout,
):
    bead_count, _, own_count = coords.shape
    ghost_width = ghost_rows.shape[1] // 2
    channels = embed.shape[1]
    onehot = (species[:, None] == jnp.arange(embed.shape[0], dtype=jnp.int32)[None, :]).astype(
        jnp.float32
    )
    h_start = jnp.dot(onehot, embed, precision=lax.Precision.HIGHEST) + atom_features
    masses = jnp.dot(onehot, jnp.array(MASSES, dtype=jnp.float32), precision=lax.Precision.HIGHEST)
    handed = (
        ghost_rows[:, :, None] == jnp.arange(own_count, dtype=jnp.int32)[None, None, :]
    ).astype(jnp.float32)
    selector = selection_table(neighbours, own_count + 2 * ghost_width)
    values_zero = jnp.dot(h_start, w_value[0].astype(jnp.float32), precision=lax.Precision.HIGHEST)
    outgoing_xyz = jnp.einsum("bga,bca->bcg", handed, coords, precision=lax.Precision.HIGHEST)
    outgoing_values = jnp.einsum(
        "bga,ac->bcg", handed, values_zero, precision=lax.Precision.HIGHEST
    )
    packed = jnp.concatenate([outgoing_xyz, outgoing_values], axis=1)
    received = padded(packed, (("space", 2),), ghost_width)
    ghosts = jnp.concatenate(
        [received[:, :, :ghost_width], received[:, :, 3 * ghost_width :]], axis=2
    )
    extended_xyz = jnp.concatenate([coords, ghosts[:, :3]], axis=2)
    values_ext = jnp.concatenate(
        [
            jnp.broadcast_to(values_zero[None], (bead_count, own_count, channels)),
            jnp.transpose(ghosts[:, 3:], (0, 2, 1)),
        ],
        axis=1,
    )
    hidden_zero = jnp.broadcast_to(h_start[None], (bead_count, own_count, channels))

    def first_layer(xyz_ext):
        return mix_layer(
            hidden_zero,
            edge_messages(values_ext, xyz_ext, neighbours, selector, w_filter[0]),
            w_out[0],
        )

    hidden_one, first_back = jax.vjp(first_layer, extended_xyz)
    values_one, value_back = jax.vjp(lambda hidden: value_rows(hidden, w_value[1]), hidden_one)
    picked = jnp.einsum("bga,bac->bgc", handed, values_one, precision=lax.Precision.HIGHEST)
    received = padded(picked.astype(jnp.bfloat16), (("space", 1),), ghost_width).astype(
        picked.dtype
    )
    ghost_values = jnp.concatenate(
        [received[:, :ghost_width], received[:, 3 * ghost_width :]], axis=1
    )

    def second_layer(hidden, own_values, far_values, xyz_ext):
        joined = jnp.concatenate([own_values, far_values], axis=1)
        hidden_two = mix_layer(
            hidden, edge_messages(joined, xyz_ext, neighbours, selector, w_filter[1]), w_out[1]
        )
        return jnp.sum(jax.nn.silu(hidden_two) * readout)

    energy_part, second_back = jax.vjp(
        second_layer, hidden_one, values_one, ghost_values, extended_xyz
    )
    feature_grad, value_grad, ghost_grad, coord_grad = second_back(jnp.ones((), jnp.float32))
    received = padded(ghost_grad.astype(jnp.bfloat16), (("space", 1),), ghost_width).astype(
        ghost_grad.dtype
    )
    arriving = jnp.concatenate([received[:, :ghost_width], received[:, 3 * ghost_width :]], axis=1)
    value_grad = value_grad + jnp.einsum(
        "bga,bgc->bac", handed, arriving, precision=lax.Precision.HIGHEST
    )
    feature_grad = feature_grad + value_back(value_grad)[0]
    coord_grad = coord_grad + first_back(feature_grad)[0]
    received = padded(coord_grad[:, :, own_count:], (("space", 2),), ghost_width)
    arriving = jnp.concatenate(
        [received[:, :, :ghost_width], received[:, :, 3 * ghost_width :]], axis=2
    )
    own_grad = coord_grad[:, :, :own_count] + jnp.einsum(
        "bga,bcg->bca", handed, arriving, precision=lax.Precision.HIGHEST
    )
    state = jnp.concatenate([coords, momenta - 0.5 * STEP_DT * own_grad], axis=1)
    total_beads = bead_count * lax.axis_size("bead")
    matrix, omegas = normal_table(total_beads)
    first_bead = lax.axis_index("bead") * bead_count
    columns = lax.dynamic_slice_in_dim(matrix, first_bead, bead_count, 1)
    weights = columns
    normal_modes = jnp.einsum(
        "jk,jcn->kcn",
        weights,
        lax.all_gather(state, "bead", axis=0, tiled=True),
        precision=lax.Precision.HIGHEST,
    )
    normal_modes = advance(
        normal_modes, lax.dynamic_slice_in_dim(omegas, first_bead, bead_count, 0), masses
    )
    mode_rows = lax.dynamic_slice_in_dim(matrix, first_bead, bead_count, 0)
    weights = mode_rows
    result = jnp.einsum(
        "jk,kcn->jcn",
        weights,
        lax.all_gather(normal_modes, "bead", axis=0, tiled=True),
        precision=lax.Precision.HIGHEST,
    )
    return (result[:, :3], result[:, 3:])


def solution(mesh):
    placed = (
        P("bead", None, "space"),
        P("bead", None, "space"),
        P("space"),
        P("space", None),
        P("bead", "space", None),
        P("bead", "space"),
        P(),
        P(),
        P(),
        P(),
        P(),
    )
    return jax.shard_map(
        local,
        mesh=mesh,
        in_specs=placed,
        out_specs=(P("bead", None, "space"), P("bead", None, "space")),
        check_vma=False,
    )
```

profile of v0, /device:TPU:32, one launch (start us, length us, event | category | flops | bytes accessed | tf_op | source)
XLA Modules:
  0.0 273.7 jit_solution(6948723411721520578)
XLA Ops:
  1.3 1.2 convolution_add_fusion.1
  5.9 4.0 %collective-permute-start.1 = (f32[2,131,128]{2,1,0:T(8,128)S(1)}, f32[2,131,128]{2,1,0:T(8,128)S(1)}, u32[]{:S(2)}, u32[]{:S(2)}) collective-permute-start(f32[2,131,128]{2,1,0:T(8,128)S(1)} %get-tuple-element.10), channel_id=1, source_target_pairs={{1,0},{2,1},{3,2},{4,3},{5,4},{6,5},{7,6},{8,7},{9,8},{10,9},{11,1... | collective-permute-start | bytes 402440 | tf_op jit(solution)/shard_map/ppermute | solution.py:24
  15.0 8.1 %multiply_reduce_fusion.2 = (f32[2,4096]{1,0:T(2,128)S(1)}, f32[2,3,4096]{2,1,0:T(4,128)S(1)}) fusion(f32[2,3,4096]{2,0,1:T(2,128)S(1)} %sub.57, s32[2,4096]{1,0:T(2,128)S(1)} %eq.73, f32[2,3,256]{2,1,0:T(4,128)S(1)} %slice.107, f32[2,3,256]{2,1,0:T(4,128)S(1)} %copy.148), kind=kOutput, calls=%fused_computation.109 | convolution fusion | flops 155257856 | bytes 274432 | tf_op jit(solution)/shard_map/jvp(bej,bcj->bce)/dot_general | solution.py:55
  23.4 7.5 %fusion.4 = f32[2,4096,128]{2,1,0:T(8,128)S(1)} fusion(s32[2,4096]{1,0:T(2,128)S(1)} %eq.73, f32[2,256,128]{1,2,0:T(8,128)S(1)} %slice_bitcast_fusion, f32[2,256,128]{1,2,0:T(8,128)S(1)} %broadcast_in_dim.76), kind=kOutput, calls=%fused_computation.5 | convolution fusion | flops 6446776320 | bytes 4751360 | tf_op jit(solution)/shard_map/jvp(bej,bjc->bec)/dot_general | solution.py:62
  31.0 8.3 %fusion.17 = bf16[2,256,128]{2,1,0:T(8,128)(2,1)S(1)} fusion(f32[2,256,16,128]{3,2,1,0:T(8,128)S(1)} %bitcast.104, f32[2,256,16]{1,2,0:T(8,128)S(1)} %compare_convert_fusion, f32[16]{0:T(128)S(1)} %iota_multiply_fusion, f32[2,256,16]{1,2,0:T(8,128)S(1)} %copy.126, f32[2,16,128]{2,1,0:T(8,128)S(1)} %copy-done.6), kind=kOutput, calls=%fused_computation.22 | convolution fusion | flops 204800000 | bytes 4399616 | tf_op jit(solution)/shard_map/jvp(bakn,nc->bakc)/dot_general | solution.py:61
  40.2 1.6 collective-permute-start.3
  42.1 1.6 collective-permute-done.3
  43.7 4.1 %collective-permute-done.2 = bf16[2,128,128]{2,1,0:T(8,128)(2,1)S(1)} collective-permute-done((bf16[2,128,128]{2,1,0:T(8,128)(2,1)S(1)}, bf16[2,128,128]{2,1,0:T(8,128)(2,1)S(1)}, u32[]{:S(2)}, u32[]{:S(2)}) %collective-permute-start.2) | collective-permute-done | bytes 65568 | tf_op jit(solution)/shard_map/ppermute | solution.py:23
  47.8 8.0 %fusion.3 = f32[2,4096,128]{2,1,0:T(8,128)S(1)} fusion(s32[2,4096]{1,0:T(2,128)S(1)} %eq.73, f32[2,128,128]{2,1,0:T(8,128)S(1)} %get-tuple-element.17, f32[2,128,128]{2,1,0:T(8,128)S(1)} %get-tuple-element.16, f32[2,256,128]{2,1,0:T(8,128)S(1)} %fusion.74), kind=kOutput, calls=%fused_computation.4 | convolution fusion | flops 6446907392 | bytes 4751360 | tf_op jit(solution)/shard_map/jvp(bej,bjc->bec)/dot_general | solution.py:62
  55.8 8.5 %fusion.15 = (bf16[2,256,128]{2,1,0:T(8,128)(2,1)S(1)}, f32[2,256,16,128]{3,1,2,0:T(8,128)S(1)}) fusion(f32[2,256,16,128]{3,2,1,0:T(8,128)S(1)} %bitcast.102, f32[2,256,16]{1,2,0:T(8,128)S(1)} %compare_convert_fusion, f32[2,16,128]{2,1,0:T(8,128)S(1)} %copy-done.6, f32[16]{0:T(128)S(1)} %iota_multiply_fusion, f32[2,256,16]{1,2,0:T(8,128)S(1)} %copy.126), kind=kOutput, calls=%fused_computation.19 | convolution fusion | flops 204800000 | bytes 8593920 | tf_op jit(solution)/shard_map/jvp(bakn,nc->bakc)/dot_general | solution.py:61
  65.0 1.4 multiply_multiply_fusion
  66.4 2.4 copy.139
  68.9 14.6 %fusion.142 = (bf16[2,512,128]{2,1,0:T(8,128)(2,1)S(1)}, f32[2,512,128]{2,1,0:T(8,128)S(1)}) fusion(f32[2,4096,128]{2,1,0:T(8,128)S(1)} %bitcast.103, s32[2,4096]{1,0:T(2,128)S(1)} %eq.73), kind=kOutput, calls=%fused_computation.200 | convolution fusion | flops 6446776320 | bytes 5013504 | tf_op jit(solution)/shard_map/transpose(jvp(bej,bjc->bec))/dot_general | solution.py:62
  85.5 4.2 %collective-permute-done.4 = bf16[2,128,128]{2,1,0:T(8,128)(2,1)S(1)} collective-permute-done((bf16[2,128,128]{2,1,0:T(8,128)(2,1)S(1)}, bf16[2,128,128]{2,1,0:T(8,128)(2,1)S(1)}, u32[]{:S(2)}, u32[]{:S(2)}) %collective-permute-start.4) | collective-permute-done | bytes 65568 | tf_op jit(solution)/shard_map/ppermute | solution.py:23
  91.0 5.4 %fusion.12 = (f32[2,4096,128]{2,1,0:T(8,128)}, f32[2,4096,128]{2,1,0:T(8,128)S(1)}) fusion(f32[2,4096,128]{2,1,0:T(8,128)} %copy-done.2, f32[2,256,128]{2,1,0:T(8,128)S(1)} %convert.9, f32[2,4096]{1,0:T(2,128)S(1)} %mul.321, f32[2,4096,128]{2,1,0:T(8,128)} %copy-done.1, f32[2,256,128]{2,1,0:T(8,128)S(1)} %convert.7), kind=kLoop, calls=%fused_computation.14 | loop fusion | flops 4194304 | bytes 17334272 | tf_op jit(solution)/shard_map/transpose(jvp())/mul | solution.py:64
  96.4 30.8 %fusion.110 = f32[2,256,16,16]{2,3,1,0:T(8,128)} fusion(f32[2,256,16,128]{3,2,1,0:T(8,128)S(1)} %bitcast.101, f32[2,16,128]{2,1,0:T(8,128)S(1)} %copy-done.6), kind=kOutput, calls=%fused_computation.155 | convolution fusion | flops 201326592 | bytes 4726784 | tf_op jit(solution)/shard_map/transpose(jvp(bakn,nc->bakc))/dot_general | solution.py:61
  127.2 4.1 %copy.133 = f32[2,256,16,16]{1,3,2,0:T(8,128)S(1)} copy(f32[2,256,16,16]{2,3,1,0:T(8,128)} %fusion.110) | data formatting | bytes 1048576 | tf_op jit(solution)/shard_map/transpose(jvp(bakn,nc->bakc))/dot_general | solution.py:61
  131.3 33.7 %fusion.113 = f32[2,256,16,16]{2,3,1,0:T(8,128)} fusion(f32[2,256,16,128]{3,2,1,0:T(8,128)} %bitcast.100, f32[2,16,128]{2,1,0:T(8,128)S(1)} %copy-done.6), kind=kOutput, calls=%fused_computation.158 | convolution fusion | flops 201326592 | bytes 4726784 | tf_op jit(solution)/shard_map/transpose(jvp(bakn,nc->bakc))/dot_general | solution.py:61
  165.0 3.7 %copy.142 = f32[2,256,16,16]{1,3,2,0:T(8,128)S(1)} copy(f32[2,256,16,16]{2,3,1,0:T(8,128)} %fusion.113) | data formatting | bytes 1048576 | tf_op jit(solution)/shard_map/transpose(jvp(bakn,nc->bakc))/dot_general | solution.py:61
  171.2 6.5 %fusion.20 = f32[2,3,512]{2,1,0:T(4,128)S(1)} fusion(s32[2,4096]{1,0:T(2,128)S(1)} %eq.73, f32[2,4096]{1,0:T(2,128)S(1)} %get-tuple-element.21, f32[2,3,256]{2,1,0:T(4,128)S(1)} %get-tuple-element.41, f32[2,3,4096]{2,1,0:T(4,128)S(1)} %get-tuple-element.36, f32[2,3,4096]{2,0,1:T(2,128)S(1)} %sub.57), kind=kOutput, calls=%fused_computation.33 | convolution fusion | flops 155266048 | bytes 280576 | tf_op jit(solution)/shard_map/transpose(jvp(bej,bcj->bce))/dot_general | solution.py:55
  177.7 6.5 %fusion.19 = f32[2,3,512]{2,1,0:T(4,128)S(1)} fusion(f32[2,3,512]{2,1,0:T(4,128)S(1)} %fusion.20, s32[2,4096]{1,0:T(2,128)S(1)} %eq.73, f32[2,4096]{1,0:T(2,128)S(1)} %get-tuple-element.20, f32[2,3,256]{2,1,0:T(4,128)S(1)} %get-tuple-element.42, f32[2,3,4096]{2,1,0:T(4,128)S(1)} %get-tuple-element.36, f32[2,3,4096]{2,0,1:T(2,128)S(1)} %sub.57), kind=kOutput, calls=%fused_computation.32 | convolution fusion | flops 155269120 | bytes 292864 | tf_op jit(solution)/shard_map/transpose(jvp(bej,bcj->bce))/dot_general | solution.py:55
  185.7 3.9 %collective-permute-done.6 = f32[2,3,128]{2,1,0:T(4,128)S(1)} collective-permute-done((f32[2,3,128]{2,1,0:T(4,128)S(1)}, f32[2,3,128]{2,1,0:T(4,128)S(1)}, u32[]{:S(2)}, u32[]{:S(2)}) %collective-permute-start.6) | collective-permute-done | bytes 3104 | tf_op jit(solution)/shard_map/ppermute | solution.py:23
  189.9 40.9 %all_gather.6 = f32[32,6,256]{2,1,0:T(8,128)S(1)} all-gather(f32[2,6,256]{2,1,0:T(8,128)S(1)} %pad_maximum_fusion.5), channel_id=1, replica_groups=mesh['bead'=16,'space'=16] {'bead'}, dimensions={0}, use_global_device_ids=true | all-gather | bytes 208896 | tf_op jit(solution)/shard_map/all_gather | solution.py:191
  231.2 41.4 %all_gather.7 = f32[32,6,256]{2,1,0:T(8,128)S(1)} all-gather(f32[2,6,256]{2,1,0:T(8,128)S(1)} %copy.150), channel_id=1, replica_groups=mesh['bead'=16,'space'=16] {'bead'}, dimensions={0}, use_global_device_ids=true | all-gather | bytes 208896 | tf_op jit(solution)/shard_map/all_gather | solution.py:202
  (99 shorter events, 19.7 us)
Async XLA Ops:
  0.6 0.7 copy-start
  5.9 9.1 %collective-permute-start = (f32[2,131,128]{2,1,0:T(8,128)S(1)}, f32[2,131,128]{2,1,0:T(8,128)S(1)}, u32[]{:S(2)}, u32[]{:S(2)}) collective-permute-start(f32[2,131,128]{2,1,0:T(8,128)S(1)} %get-tuple-element.11), channel_id=1, source_target_pairs={{0,1},{1,2},{2,3},{3,4},{4,5},{5,6},{6,7},{7,8},{8,9},{9,10},{10,1... | collective-permute-start | bytes 402440 | tf_op jit(solution)/shard_map/ppermute | solution.py:23
  5.9 9.0 %collective-permute-start.1 = (f32[2,131,128]{2,1,0:T(8,128)S(1)}, f32[2,131,128]{2,1,0:T(8,128)S(1)}, u32[]{:S(2)}, u32[]{:S(2)}) collective-permute-start(f32[2,131,128]{2,1,0:T(8,128)S(1)} %get-tuple-element.10), channel_id=1, source_target_pairs={{1,0},{2,1},{3,2},{4,3},{5,4},{6,5},{7,6},{8,7},{9,8},{10,9},{11,1... | collective-permute-start | bytes 402440 | tf_op jit(solution)/shard_map/ppermute | solution.py:24
  23.4 7.5 %copy-start.6 = (f32[2,16,128]{2,1,0:T(8,128)S(1)}, f32[2,16,128]{2,1,0:T(8,128)}, u32[]{:S(2)}) copy-start(f32[2,16,128]{2,1,0:T(8,128)} %param.19) | copy-start | bytes 49156
  30.9 16.9 %copy-start.2 = (f32[2,4096,128]{2,1,0:T(8,128)}, f32[2,4096,128]{2,1,0:T(8,128)S(1)}, u32[]{:S(2)}) copy-start(f32[2,4096,128]{2,1,0:T(8,128)S(1)} %fusion.4) | copy-start | bytes 12582916
  30.9 8.4 %copy-start.3 = (bf16[2,128,128]{2,1,0:T(8,128)(2,1)S(1)}, bf16[2,128,128]{2,1,0:T(8,128)(2,1)}, u32[]{:S(2)}) copy-start(bf16[2,128,128]{2,1,0:T(8,128)(2,1)} %param.21) | copy-start | bytes 196612
  30.9 8.6 %copy-start.4 = (bf16[2,128,128]{2,1,0:T(8,128)(2,1)S(1)}, bf16[2,128,128]{2,1,0:T(8,128)(2,1)}, u32[]{:S(2)}) copy-start(bf16[2,128,128]{2,1,0:T(8,128)(2,1)} %param.20) | copy-start | bytes 196612
  31.0 8.8 %copy-start.7 = (s32[2,256]{1,0:T(2,128)S(1)}, s32[2,256]{1,0:T(2,128)}, u32[]{:S(2)}) copy-start(s32[2,256]{1,0:T(2,128)} %param.17) | copy-start | bytes 6148
  40.2 3.5 %collective-permute-start.3 = (bf16[2,128,128]{2,1,0:T(8,128)(2,1)S(1)}, bf16[2,128,128]{2,1,0:T(8,128)(2,1)S(1)}, u32[]{:S(2)}, u32[]{:S(2)}) collective-permute-start(bf16[2,128,128]{2,1,0:T(8,128)(2,1)S(1)} %get-tuple-element.19), channel_id=1, source_target_pairs={{1,0},{2,1},{3,2},{4,3},{5,4},{6,5},{7,6},{8,7},{9,8},{10,9},{11,1... | collective-permute-start | bytes 196616 | tf_op jit(solution)/shard_map/ppermute | solution.py:24
  41.8 6.0 %collective-permute-start.2 = (bf16[2,128,128]{2,1,0:T(8,128)(2,1)S(1)}, bf16[2,128,128]{2,1,0:T(8,128)(2,1)S(1)}, u32[]{:S(2)}, u32[]{:S(2)}) collective-permute-start(bf16[2,128,128]{2,1,0:T(8,128)(2,1)S(1)} %get-tuple-element.18), channel_id=1, source_target_pairs={{0,1},{1,2},{2,3},{3,4},{4,5},{5,6},{6,7},{7,8},{8,9},{9,10},{10,1... | collective-permute-start | bytes 196616 | tf_op jit(solution)/shard_map/ppermute | solution.py:23
  55.8 8.5 %copy-start.1 = (f32[2,4096,128]{2,1,0:T(8,128)}, f32[2,4096,128]{2,1,0:T(8,128)S(1)}, u32[]{:S(2)}) copy-start(f32[2,4096,128]{2,1,0:T(8,128)S(1)} %fusion.3) | copy-start | bytes 12582916
  55.8 8.5 %copy-start.9 = (f32[128]{0:T(128)S(1)}, f32[128]{0:T(128)}, u32[]{:S(2)}) copy-start(f32[128]{0:T(128)} %param.22) | copy-start | bytes 1540
  83.5 2.0 collective-permute-start.5
  83.6 6.1 %collective-permute-start.4 = (bf16[2,128,128]{2,1,0:T(8,128)(2,1)S(1)}, bf16[2,128,128]{2,1,0:T(8,128)(2,1)S(1)}, u32[]{:S(2)}, u32[]{:S(2)}) collective-permute-start(bf16[2,128,128]{2,1,0:T(8,128)(2,1)S(1)} %get-tuple-element.14), channel_id=1, source_target_pairs={{0,1},{1,2},{2,3},{3,4},{4,5},{5,6},{6,7},{7,8},{8,9},{9,10},{10,1... | collective-permute-start | bytes 196616 | tf_op jit(solution)/shard_map/ppermute | solution.py:23
  165.0 5.4 %copy-start.5 = (f32[2,3,256]{2,0,1:T(2,128)S(1)}, f32[2,3,256]{2,0,1:T(2,128)}, u32[]{:S(2)}) copy-start(f32[2,3,256]{2,0,1:T(2,128)} %param.12) | copy-start | bytes 18436
  177.7 11.8 %copy-start.8 = (f32[2,3,256]{2,0,1:T(2,128)S(1)}, f32[2,3,256]{2,0,1:T(2,128)}, u32[]{:S(2)}) copy-start(f32[2,3,256]{2,0,1:T(2,128)} %param.13) | copy-start | bytes 18436
  184.3 1.4 collective-permute-start.7
  184.3 5.2 %collective-permute-start.6 = (f32[2,3,128]{2,1,0:T(4,128)S(1)}, f32[2,3,128]{2,1,0:T(4,128)S(1)}, u32[]{:S(2)}, u32[]{:S(2)}) collective-permute-start(f32[2,3,128]{2,1,0:T(4,128)S(1)} %get-tuple-element.27), channel_id=1, source_target_pairs={{0,1},{1,2},{2,3},{3,4},{4,5},{5,6},{6,7},{7,8},{8,9},{9,10},{10,1... | collective-permute-start | bytes 9224 | tf_op jit(solution)/shard_map/ppermute | solution.py:23
where the time goes:
time: 277 us; the launch traced here: 274 us
  matrix products  141 us (51%)
  blocking collectives  82.3 us (30%)
  local copies, waits for them, and re-layouts  16.9 us (6%)
  waiting for transfers between devices  15 us (5%)
  other arithmetic  9.63 us (3%)
  starting transfers between devices  7.22 us (3%)
    dot_general x4, matrix products, edge_messages(): jnp.einsum('bakn,nc->bakc', radial, w_radial, precision=lax.Precision.HIG...  81.3 us
    all_gather x1, blocking collectives, local(): lax.all_gather(normal_modes, 'bead', axis=0, tiled=True)  41.4 us
    all_gather x1, blocking collectives, local(): lax.all_gather(state, 'bead', axis=0, tiled=True)  40.9 us
    dot_general x3, matrix products, edge_messages(): jnp.einsum('bej,bjc->bec', selector, values, precision=lax.Precision.HIGH...  30.1 us
    dot_general x3, matrix products, edge_messages(): jnp.einsum('bej,bcj->bce', selector, positions, precision=lax.Precision.H...  21.1 us
    ppermute x4, waiting for transfers between devices, padded(): before = lax.ppermute(last, axis, up)  12.2 us
    dot_general x2, local copies, waits for them, and re-layouts, edge_messages(): jnp.einsum('bakn,nc->bakc', radial, w_radial, precision=lax.Precision.HIG...  7.89 us
    mul x2, other arithmetic, edge_messages(): return jnp.sum(filters * far_values * present[..., None], axis=2)  6.87 us
  transfers between devices with their start and end apart: 8, of which 6 were waited for; matrix products, arithmetic and copies ran while one was open for 2% of the time, Pallas kernels for 0%

commit v1 on v0

v1 whole, which is shorter than its diff:
```python
import functools
import math

import jax
import jax.numpy as jnp
from jax import lax
from jax.experimental import pallas as pl
from jax.experimental.pallas import tpu as pltpu
from jax.sharding import PartitionSpec as P

MASSES = (1.008, 12.011, 14.007, 15.999, 30.974)
STEP_DT = 1.0
OMEGA_P = 0.6
WIDTH = 3.125
SPACING = 0.25
SOFTEN = 0.01

MESH = pl.DeviceIdType.MESH
BF16 = jnp.bfloat16
F32 = jnp.float32
GROUP = 4


def dot(a, b):
    return jnp.dot(a, b, preferred_element_type=F32)


def dot_nt(a, b):
    return lax.dot_general(a, b, (((1,), (1,)), ((), ())), preferred_element_type=F32)


def split(x):
    hi = x.astype(BF16)
    return hi, (x - hi.astype(F32)).astype(BF16)


def stacked(x):
    hi, lo = split(x)
    return jnp.concatenate([hi, lo, hi], axis=0)


def ring_tables(count):
    omegas = [2.0 * OMEGA_P * math.sin(math.pi * k / count) for k in range(count)]

    def kernel_of(g):
        return [
            sum(g(w) * math.cos(2.0 * math.pi * k * d / count) for k, w in enumerate(omegas)) / count
            for d in range(count)
        ]

    keep = kernel_of(lambda w: math.cos(w * STEP_DT))
    drift = kernel_of(lambda w: math.sin(w * STEP_DT) / w if w > 0.0 else STEP_DT)
    spring = kernel_of(lambda w: w * math.sin(w * STEP_DT))
    return keep, drift, spring


def kernel(
    n_bead,
    n_space,
    coords,
    momenta,
    species,
    feats,
    nbr,
    ghost_rows,
    embed,
    w_filter,
    w_value,
    w_out,
    readout,
    out_q,
    out_p,
    sel,
    handed,
    pos,
    text,
    halo0_out,
    halo0_in,
    halo1_out,
    halo1_in,
    grad_out,
    grad_in,
    pgrad_out,
    pgrad_in,
    state,
    force,
    offs,
    rads,
    gv,
    p0,
    f1,
    f1d,
    g1,
    msum,
    h0,
    h1,
    u0,
    v1,
    back,
    dh,
    dms,
    drs,
    dv,
    dpos,
    fown,
    halo_send,
    halo_recv,
    state_send,
    state_recv,
    force_send,
    force_recv,
):
    beads, atoms = 2, coords.shape[2]
    ghosts = ghost_rows.shape[1] // 2
    channels = feats.shape[1]
    slots = nbr.shape[1]
    groups = slots // GROUP
    wide = GROUP * atoms
    me_b = lax.axis_index("bead")
    me_s = lax.axis_index("space")
    left = lax.rem(me_s + n_space - 1, n_space)
    right = lax.rem(me_s + 1, n_space)

    barrier = pltpu.get_barrier_semaphore()
    for side in (left, right):
        pl.semaphore_signal(barrier, inc=1, device_id={"space": side}, device_id_type=MESH)
    for o in range(1, n_bead):
        peer = lax.rem(me_b + o, n_bead)
        pl.semaphore_signal(barrier, inc=1, device_id={"bead": peer}, device_id_type=MESH)

    def to_side(number, src, dst_in, going_left):
        mine, theirs = (0, 1) if going_left else (1, 0)
        return pltpu.make_async_remote_copy(
            src_ref=src.at[mine],
            dst_ref=dst_in.at[theirs],
            send_sem=halo_send.at[number, mine],
            recv_sem=halo_recv.at[number, theirs],
            device_id={"space": left if going_left else right},
            device_id_type=MESH,
        )

    def both_sides(number, src, dst_in):
        return [to_side(number, src, dst_in, True), to_side(number, src, dst_in, False)]

    def to_beads(src, buffer, send, recv):
        return [
            pltpu.make_async_remote_copy(
                src_ref=src,
                dst_ref=buffer.at[o],
                send_sem=send.at[o],
                recv_sem=recv.at[o],
                device_id={"bead": lax.rem(me_b + o, n_bead)},
                device_id_type=MESH,
            )
            for o in range(1, n_bead)
        ]

    kinds = species[...]
    start = jnp.transpose(feats[...])
    mass = jnp.zeros((1, atoms), F32)
    for e in range(embed.shape[0]):
        column = jnp.transpose(jnp.broadcast_to(embed[e : e + 1, :], (128, channels)))
        column = jnp.concatenate([column] * (atoms // 128), axis=1)
        start = start + jnp.where(kinds == e, column, 0.0)
        mass = jnp.where(kinds == e, MASSES[e], mass)
    h0[...] = start
    hi, lo = split(start)
    wv0_t = jnp.transpose(w_value[0].astype(F32)).astype(BF16)
    values_zero = (dot(wv0_t, hi) + dot(wv0_t, lo)).astype(BF16)

    pos[...] = jnp.zeros_like(pos)
    for b in range(beads):
        for c in range(3):
            pos[b, c : c + 1, :] = coords[c, b : b + 1, :]
    atom_rows = lax.broadcasted_iota(jnp.int32, (atoms, 2 * ghosts), 0)
    for b in range(beads):
        handed[b] = jnp.where(ghost_rows[b : b + 1, :] == atom_rows, 1.0, 0.0).astype(BF16)
        hi, lo = split(pos[b])
        table = jnp.concatenate([values_zero, hi, lo], axis=0)
        text[b, :, :atoms] = table
        picked = dot(table, handed[b]).astype(BF16)
        halo0_out[0, b] = picked[:, :ghosts]
        halo0_out[1, b] = picked[:, ghosts:]
    state[0, 0:8, :] = pos[0] + pltpu.roll(pos[1], 4, 0)
    state[0, 8:16, :] = jnp.zeros((8, atoms), F32)
    for b in range(beads):
        for c in range(3):
            row = 8 + 4 * b + c
            state[0, row : row + 1, :] = momenta[c, b : b + 1, :]

    pl.semaphore_wait(barrier, 2 + n_bead - 1)
    halo0 = both_sides(0, halo0_out, halo0_in)
    for copy in halo0:
        copy.start()
    state_copies = to_beads(state.at[0], state, state_send, state_recv)
    for copy in state_copies:
        copy.start()

    ext_rows = lax.broadcasted_iota(jnp.int32, (2 * atoms, atoms), 0)

    def select(q, carry):
        b, group = q // groups, lax.rem(q, groups)
        for s in range(GROUP):
            row = nbr[b, pl.ds(group * GROUP + s, 1), :]
            sel[q, :, s * atoms : (s + 1) * atoms] = jnp.where(ext_rows == row, 1.0, 0.0).astype(BF16)
        return carry

    lax.fori_loop(0, beads * groups, select, 0)

    def filter_rows(layer):
        hi, lo = split(jnp.transpose(w_filter[layer]))
        return jnp.concatenate([hi, hi, lo], axis=1)

    def transposed(weight):
        return jnp.transpose(weight.astype(F32)).astype(BF16)

    wf = [filter_rows(0), filter_rows(1)]
    wv1_t = transposed(w_value[1])
    wo_t = [transposed(w_out[0]), transposed(w_out[1])]
    read = jnp.transpose(jnp.broadcast_to(readout[...], (128, channels)))
    read = jnp.concatenate([read] * (atoms // 128), axis=1)
    msum[...] = jnp.zeros_like(msum)
    dv[...] = jnp.zeros_like(dv)
    dpos[...] = jnp.zeros_like(dpos)
    fown[...] = jnp.zeros_like(fown)

    for copy in halo0:
        copy.wait_recv()
    for b in range(beads):
        text[b, :, atoms : atoms + ghosts] = halo0_in[0, b]
        text[b, :, atoms + ghosts :] = halo0_in[1, b]

    centers = SPACING * lax.broadcasted_iota(jnp.int32, (16, atoms), 0).astype(F32)

    def layer_zero(q, carry):
        b = q // groups
        got = dot(text[b], sel[q])
        gv[q] = got[:channels]
        acc = jnp.zeros((channels, atoms), F32)
        for s in range(GROUP):
            here = slice(s * atoms, (s + 1) * atoms)
            off = got[channels : channels + 8, here] + got[channels + 8 :, here] - pos[b]
            offs[q, 0:8, here] = off
            square = jnp.sum(off * off, axis=0, keepdims=True) + SOFTEN
            inverse = lax.rsqrt(square)
            offs[q, 8:16, here] = jnp.broadcast_to(inverse, (8, atoms))
            t = square * inverse - centers
            rad = jnp.exp(-WIDTH * (t * t))
            rads[q, 0, :, here] = stacked(rad)
            rads[q, 1, :, here] = stacked((-2.0 * WIDTH) * (t * rad))
            acc = acc + dot(wf[0], rads[q, 0, :, here]) * gv[q, :, here]
        msum[0, b] += acc
        return carry

    lax.fori_loop(0, beads * groups, layer_zero, 0)

    for b in range(beads):
        update = dot(wo_t[0], msum[0, b].astype(BF16))
        u0[b] = update
        hidden = h0[...] + update * jax.nn.sigmoid(update)
        h1[b] = hidden
        value = dot(wv1_t, hidden.astype(BF16)).astype(BF16)
        v1[b] = value
        picked = dot(value, handed[b]).astype(BF16)
        halo1_out[0, b] = picked[:, :ghosts]
        halo1_out[1, b] = picked[:, ghosts:]
    halo1 = both_sides(1, halo1_out, halo1_in)
    for copy in halo1:
        copy.start()

    def between(q, carry):
        b = q // groups
        g1[q] = dot(v1[b], sel[q, :atoms, :])
        for s in range(GROUP):
            here = slice(s * atoms, (s + 1) * atoms)
            p0[q, :, here] = dot(wf[0], rads[q, 1, :, here]) * gv[q, :, here]
            f1[q, :, here] = dot(wf[1], rads[q, 0, :, here])
            f1d[q, :, here] = dot(wf[1], rads[q, 1, :, here])
        return carry

    lax.fori_loop(0, beads * groups, between, 0)

    for copy in halo1:
        copy.wait_recv()

    def layer_one(q, carry):
        b = q // groups
        far = jnp.concatenate([halo1_in[0, b], halo1_in[1, b]], axis=1)
        got = dot(far, sel[q, atoms:, :])
        acc = jnp.zeros((channels, atoms), F32)
        for s in range(GROUP):
            here = slice(s * atoms, (s + 1) * atoms)
            value = g1[q, :, here] + got[:, here]
            acc = acc + f1[q, :, here] * value
            g1[q, :, here] = f1d[q, :, here] * value
        msum[1, b] += acc
        return carry

    lax.fori_loop(0, beads * groups, layer_one, 0)

    def slope(x, gate):
        return gate * (1.0 + x * (1.0 - gate))

    for b in range(beads):
        update = dot(wo_t[1], msum[1, b].astype(BF16))
        gate = jax.nn.sigmoid(update)
        hidden = h1[b] + update * gate
        grad = read * slope(hidden, jax.nn.sigmoid(hidden))
        dh[b] = grad
        grad = grad * slope(update, gate)
        dms[b] = dot(w_out[1], grad.astype(BF16))

    def ghost_scatter(q, carry):
        b = q // groups
        for s in range(GROUP):
            here = slice(s * atoms, (s + 1) * atoms)
            back[q, :, here] = (f1[q, :, here] * dms[b]).astype(BF16)
        dv[1, b] += dot_nt(back[q], sel[q, atoms:, :])
        return carry

    lax.fori_loop(0, beads * groups, ghost_scatter, 0)
    for b in range(beads):
        value = dv[1, b].astype(BF16)
        grad_out[0, b] = value[:, :ghosts]
        grad_out[1, b] = value[:, ghosts:]
    grads = both_sides(2, grad_out, grad_in)
    for copy in grads:
        copy.start()

    def own_scatter(q, carry):
        b = q // groups
        dv[0, b] += dot_nt(back[q], sel[q, :atoms, :])
        for s in range(GROUP):
            here = slice(s * atoms, (s + 1) * atoms)
            drs[q, :, here] = jnp.sum(dms[b] * g1[q, :, here], axis=0, keepdims=True)
        return carry

    lax.fori_loop(0, beads * groups, own_scatter, 0)

    for copy in grads:
        copy.wait_recv()
    for b in range(beads):
        arrived = jnp.concatenate([grad_in[0, b], grad_in[1, b]], axis=1)
        value = dv[0, b] + dot_nt(arrived, handed[b])
        grad = dh[b] + dot(w_value[1], value.astype(BF16))
        update = u0[b]
        grad = grad * slope(update, jax.nn.sigmoid(update))
        dms[b] = dot(w_out[0], grad.astype(BF16))

    def position_scatter(q, carry):
        b = q // groups
        parts = []
        acc = jnp.zeros((8, atoms), F32)
        for s in range(GROUP):
            here = slice(s * atoms, (s + 1) * atoms)
            slot = drs[q, :, here] + jnp.sum(dms[b] * p0[q, :, here], axis=0, keepdims=True)
            part = offs[q, 0:8, here] * offs[q, 8:16, here] * slot
            acc = acc + part
            parts.append(jnp.concatenate(split(part), axis=0))
        fown[b] += acc
        dpos[b] += dot_nt(jnp.concatenate(parts, axis=1), sel[q])
        return carry

    lax.fori_loop(0, beads * groups, position_scatter, 0)
    for b in range(beads):
        total = dpos[b, 0:8, :] + dpos[b, 8:16, :]
        fown[b] = total[:, :atoms] - fown[b]
        pgrad_out[0, b] = total[:, atoms : atoms + ghosts]
        pgrad_out[1, b] = total[:, atoms + ghosts :]
    pgrads = both_sides(3, pgrad_out, pgrad_in)
    for copy in pgrads:
        copy.start()

    keep, drift, spring = ring_tables(2 * n_bead)
    lower = lax.broadcasted_iota(jnp.int32, (8, atoms), 0) >= 4

    def spread(table, sources):
        same = jnp.zeros((8, atoms), F32)
        other = jnp.zeros((8, atoms), F32)
        count = len(table)
        for o, source in enumerate(sources):
            same = same + table[(2 * o) % count] * source
            other = other + jnp.where(lower, table[(2 * o - 1) % count], table[(2 * o + 1) % count]) * source
        return same + pltpu.roll(other, 4, 0)

    for copy in state_copies:
        copy.wait_recv()
    q_all = [state[o, 0:8, :] for o in range(n_bead)]
    p_all = [state[o, 8:16, :] for o in range(n_bead)]
    q_next = spread(keep, q_all) + spread(drift, p_all) / mass
    p_next = spread(keep, p_all) - mass * spread(spring, q_all)

    for copy in pgrads:
        copy.wait_recv()
    for b in range(beads):
        arrived = jnp.concatenate([pgrad_in[0, b], pgrad_in[1, b]], axis=1)
        placed = dot_nt(jnp.concatenate(split(arrived), axis=0), handed[b])
        fown[b] = (-0.5 * STEP_DT) * (fown[b] + placed[:8] + placed[8:])
    force[0] = fown[0] + pltpu.roll(fown[1], 4, 0)
    force_copies = to_beads(force.at[0], force, force_send, force_recv)
    for copy in force_copies:
        copy.start()
    for copy in force_copies:
        copy.wait_recv()
    kicks = [force[o] for o in range(n_bead)]
    q_next = q_next + spread(drift, kicks) / mass
    p_next = p_next + spread(keep, kicks)
    for b in range(beads):
        for c in range(3):
            row = 4 * b + c
            out_q[c, b : b + 1, :] = q_next[row : row + 1, :]
            out_p[c, b : b + 1, :] = p_next[row : row + 1, :]
    for copy in halo0 + halo1 + grads + pgrads + state_copies + force_copies:
        copy.wait_send()


def local(
    coords,
    momenta,
    species,
    atom_features,
    neighbours,
    ghost_rows,
    embed,
    w_filter,
    w_value,
    w_out,
    readout,
):
    n_bead, n_space = lax.axis_size("bead"), lax.axis_size("space")
    beads, _, atoms = coords.shape
    slots = neighbours.shape[2]
    ghosts = ghost_rows.shape[1] // 2
    channels = embed.shape[1]
    steps = beads * slots // GROUP
    wide = GROUP * atoms
    rows = channels + 16
    vmem = pl.BlockSpec(memory_space=pltpu.VMEM)
    big = pltpu.VMEM((steps, channels, wide), F32)
    per_bead = pltpu.VMEM((beads, channels, atoms), F32)
    shape = jax.ShapeDtypeStruct((3, beads, atoms), F32)
    q_next, p_next = pl.pallas_call(
        functools.partial(kernel, n_bead, n_space),
        out_shape=(shape, shape),
        in_specs=[vmem] * 11,
        out_specs=(vmem, vmem),
        scratch_shapes=[
            pltpu.VMEM((steps, 2 * atoms, wide), BF16),
            pltpu.VMEM((beads, atoms, 2 * ghosts), BF16),
            pltpu.VMEM((beads, 8, atoms), F32),
            pltpu.VMEM((beads, rows, 2 * atoms), BF16),
            pltpu.VMEM((2, beads, rows, ghosts), BF16),
            pltpu.VMEM((2, beads, rows, ghosts), BF16),
            pltpu.VMEM((2, beads, channels, ghosts), BF16),
            pltpu.VMEM((2, beads, channels, ghosts), BF16),
            pltpu.VMEM((2, beads, channels, ghosts), BF16),
            pltpu.VMEM((2, beads, channels, ghosts), BF16),
            pltpu.VMEM((2, beads, 8, ghosts), F32),
            pltpu.VMEM((2, beads, 8, ghosts), F32),
            pltpu.VMEM((n_bead, 16, atoms), F32),
            pltpu.VMEM((n_bead, 8, atoms), F32),
            pltpu.VMEM((steps, 16, wide), F32),
            pltpu.VMEM((steps, 2, 48, wide), BF16),
            big,
            big,
            big,
            big,
            big,
            pltpu.VMEM((2, beads, channels, atoms), F32),
            pltpu.VMEM((channels, atoms), F32),
            per_bead,
            per_bead,
            pltpu.VMEM((beads, channels, atoms), BF16),
            pltpu.VMEM((steps, channels, wide), BF16),
            per_bead,
            per_bead,
            pltpu.VMEM((steps, 1, wide), F32),
            pltpu.VMEM((2, beads, channels, atoms), F32),
            pltpu.VMEM((beads, 16, 2 * atoms), F32),
            pltpu.VMEM((beads, 8, atoms), F32),
            pltpu.SemaphoreType.DMA((4, 2)),
            pltpu.SemaphoreType.DMA((4, 2)),
            pltpu.SemaphoreType.DMA((n_bead,)),
            pltpu.SemaphoreType.DMA((n_bead,)),
            pltpu.SemaphoreType.DMA((n_bead,)),
            pltpu.SemaphoreType.DMA((n_bead,)),
        ],
        compiler_params=pltpu.CompilerParams(
            collective_id=0, has_side_effects=True, vmem_limit_bytes=58 * 1024 * 1024
        ),
    )(
        jnp.transpose(coords, (1, 0, 2)),
        jnp.transpose(momenta, (1, 0, 2)),
        species.reshape(1, atoms),
        atom_features,
        jnp.transpose(neighbours, (0, 2, 1)),
        ghost_rows,
        embed,
        w_filter,
        w_value,
        w_out,
        readout.reshape(1, channels),
    )
    return jnp.transpose(q_next, (1, 0, 2)), jnp.transpose(p_next, (1, 0, 2))


def solution(mesh):
    placed = (
        P("bead", None, "space"),
        P("bead", None, "space"),
        P("space"),
        P("space", None),
        P("bead", "space", None),
        P("bead", "space"),
        P(),
        P(),
        P(),
        P(),
        P(),
    )
    return jax.shard_map(
        local,
        mesh=mesh,
        in_specs=placed,
        out_specs=(P("bead", None, "space"), P("bead", None, "space")),
        check_vma=False,
    )
```

time: 277 us -> 49.7 us (0.18); the launches traced: 274 us -> 49.2 us
  matrix products: 141 us -> 0 us
  blocking collectives: 82.3 us -> 0 us
  Pallas kernels: 0 us -> 46.6 us
  waiting for transfers between devices: 15 us -> 0 us
  local copies, waits for them, and re-layouts: 16.9 us -> 1.97 us
  other arithmetic: 9.63 us -> 0 us
  starting transfers between devices: 7.22 us -> 0 us
    dot_general x26 -> x0, matrix products: 141 us -> none  [the longest x4 81.3 us: edge_messages(): jnp.einsum('bakn,nc->bakc', radial, w_radial, precision=lax.Precision.HIG...]
    all_gather x2 -> x0, blocking collectives: 82.3 us -> none  [the longest x1 41.4 us: local(): lax.all_gather(normal_modes, 'bead', axis=0, tiled=True)]
    pallas_call x0 -> x1, Pallas kernels: none -> 46.6 us  [local(): pl.pallas_call(functools.partial(kernel, n_bead, n_space), out_shape=(sha...]
    ppermute x8 -> x0, waiting for transfers between devices: 15 us -> none  [the longest x4 12.2 us: padded(): before = lax.ppermute(last, axis, up)]
    dot_general x3 -> x0, local copies, waits for them, and re-layouts: 7.97 us -> none  [the longest x2 7.89 us: edge_messages(): jnp.einsum('bakn,nc->bakc', radial, w_radial, precision=lax.Precision.HIG...]
    ppermute x8 -> x0, starting transfers between devices: 7.22 us -> none  [the longest x4 5.76 us: padded(): after = lax.ppermute(initial, axis, down)]
    mul x8 -> x0, other arithmetic: 7.06 us -> none  [the longest x2 6.87 us: edge_messages(): return jnp.sum(filters * far_values * present[..., None], axis=2)]
    mul x4 -> x0, local copies, waits for them, and re-layouts: 2.84 us -> none  [the longest x2 2.59 us: edge_messages(): return jnp.sum(filters * far_values * present[..., None], axis=2)]
  transfers between devices with their start and end apart: 8 -> 0, of which waited for: 6 -> 0; matrix products, arithmetic and copies ran while one was open for 2% -> 0% of each run, Pallas kernels for 0% -> 0%
where the time goes in v1:
time: 49.7 us; the launch traced here: 49.2 us
  Pallas kernels  46.6 us (94%)
  local copies, waits for them, and re-layouts  1.97 us (4%)
  between operations  0.65 us (1%)
    pallas_call x1, Pallas kernels, local(): pl.pallas_call(functools.partial(kernel, n_bead, n_space), out_shape=(sha...  46.6 us
    unnamed x6, local copies, waits for them, and re-layouts  1.97 us

profile of v1, /device:TPU:32, one launch (start us, length us, event | category | flops | bytes accessed | tf_op | source)
XLA Modules:
  0.0 49.2 jit_solution(4314138695979265071)
XLA Ops:
  0.6 46.6 %shard_map.122 = (f32[3,2,256]{2,1,0:T(2,128)}, f32[3,2,256]{2,1,0:T(2,128)}) custom-call(f32[3,2,256]{2,1,0:T(2,128)} %bitcast.10, f32[3,2,256]{2,1,0:T(2,128)} %bitcast.11, s32[1,256]{1,0:T(1,128)} %bitcast.12, f32[256,128]{1,0:T(8,128)} %feats.1, s32[2,16,256]{2,1,0:T(8,128)} %bitcast.7, s32[2,256]{1,0:T(2,128)} %ghost_rows.1, f32[5,128]{1,0:T(8,128)} %embed.1, ...), custom_call_target="tpu_custom_call" | custom-call | tf_op jit(solution)/shard_map/pallas_call | solution.py:442
  47.2 0.0 copy-start.1
  47.2 0.7 %copy-done.1 = f32[3,2,256]{2,1,0:T(2,128)S(1)} copy-done((f32[3,2,256]{2,1,0:T(2,128)S(1)}, f32[3,2,256]{2,1,0:T(2,128)}, u32[]{:S(2)}) %copy-start.1) | copy-done | bytes 6168
  47.9 0.0 copy-start
  47.9 0.6 %copy.15 = f32[2,3,256]{2,0,1:T(2,128)} copy(f32[2,3,256]{2,0,1:T(2,128)S(1)} %bitcast.9) | data formatting | bytes 12288
  48.5 0.1 copy-done
  48.6 0.6 %copy.16 = f32[2,3,256]{2,0,1:T(2,128)} copy(f32[2,3,256]{2,0,1:T(2,128)S(1)} %bitcast.8) | data formatting | bytes 12288
Async XLA Ops:
  47.2 0.7 %copy-start.1 = (f32[3,2,256]{2,1,0:T(2,128)S(1)}, f32[3,2,256]{2,1,0:T(2,128)}, u32[]{:S(2)}) copy-start(f32[3,2,256]{2,1,0:T(2,128)} %get-tuple-element.4) | copy-start | bytes 18436
  47.9 0.7 %copy-start = (f32[3,2,256]{2,1,0:T(2,128)S(1)}, f32[3,2,256]{2,1,0:T(2,128)}, u32[]{:S(2)}) copy-start(f32[3,2,256]{2,1,0:T(2,128)} %get-tuple-element.5) | copy-start | bytes 18436

commit v2 on v1

v2 whole, which is shorter than its diff:
```python
import functools
import math

import jax
import jax.numpy as jnp
from jax import lax
from jax.experimental import pallas as pl
from jax.experimental.pallas import tpu as pltpu
from jax.sharding import PartitionSpec as P

MASSES = (1.008, 12.011, 14.007, 15.999, 30.974)
STEP_DT = 1.0
OMEGA_P = 0.6
WIDTH = 3.125
SPACING = 0.25
SOFTEN = 0.01

MESH = pl.DeviceIdType.MESH
BF16 = jnp.bfloat16
F32 = jnp.float32
GROUP = 4


def dot(a, b):
    return jnp.dot(a, b, preferred_element_type=F32)


def dot_nt(a, b):
    return lax.dot_general(a, b, (((1,), (1,)), ((), ())), preferred_element_type=F32)


def split(x):
    hi = x.astype(BF16)
    return hi, (x - hi.astype(F32)).astype(BF16)


def stacked(x):
    hi, lo = split(x)
    return jnp.concatenate([hi, lo, hi], axis=0)


def ring_tables(count):
    omegas = [2.0 * OMEGA_P * math.sin(math.pi * k / count) for k in range(count)]

    def kernel_of(g):
        return [
            sum(g(w) * math.cos(2.0 * math.pi * k * d / count) for k, w in enumerate(omegas)) / count
            for d in range(count)
        ]

    keep = kernel_of(lambda w: math.cos(w * STEP_DT))
    drift = kernel_of(lambda w: math.sin(w * STEP_DT) / w if w > 0.0 else STEP_DT)
    spring = kernel_of(lambda w: w * math.sin(w * STEP_DT))
    return keep, drift, spring


def kernel(
    n_bead,
    n_space,
    coords,
    momenta,
    species,
    feats,
    nbr,
    ghost_rows,
    embed,
    w_filter,
    w_value,
    w_out,
    readout,
    out_q,
    out_p,
    sel,
    handed,
    pos,
    text,
    halo0_out,
    halo0_in,
    halo1_out,
    halo1_in,
    grad_out,
    grad_in,
    pgrad_out,
    pgrad_in,
    state,
    force,
    offs,
    rads,
    gv,
    p0,
    f1,
    f1d,
    g1,
    h0,
    h1,
    u0,
    v1,
    back,
    parts,
    dh,
    dms,
    drs,
    dv,
    fown,
    halo_send,
    halo_recv,
    state_send,
    state_recv,
    force_send,
    force_recv,
):
    beads, atoms = 2, coords.shape[2]
    ghosts = ghost_rows.shape[1] // 2
    channels = feats.shape[1]
    slots = nbr.shape[1]
    groups = slots // GROUP
    wide = GROUP * atoms
    me_b = lax.axis_index("bead")
    me_s = lax.axis_index("space")
    left = lax.rem(me_s + n_space - 1, n_space)
    right = lax.rem(me_s + 1, n_space)

    barrier = pltpu.get_barrier_semaphore()
    for side in (left, right):
        pl.semaphore_signal(barrier, inc=1, device_id={"space": side}, device_id_type=MESH)
    for o in range(1, n_bead):
        peer = lax.rem(me_b + o, n_bead)
        pl.semaphore_signal(barrier, inc=1, device_id={"bead": peer}, device_id_type=MESH)

    def both_sides(number, b, src, dst):
        return [
            pltpu.make_async_remote_copy(
                src_ref=src.at[b, mine],
                dst_ref=dst.at[b, 1 - mine],
                send_sem=halo_send.at[number, b, mine],
                recv_sem=halo_recv.at[number, b, 1 - mine],
                device_id={"space": side},
                device_id_type=MESH,
            )
            for mine, side in enumerate((left, right))
        ]

    def to_beads(buffer, part, send, recv):
        return [
            pltpu.make_async_remote_copy(
                src_ref=part(buffer, 0),
                dst_ref=part(buffer, o),
                send_sem=send.at[o],
                recv_sem=recv.at[o],
                device_id={"bead": lax.rem(me_b + o, n_bead)},
                device_id_type=MESH,
            )
            for o in range(1, n_bead)
        ]

    def start_all(copies):
        for copy in copies:
            copy.start()

    def arrive(copies):
        for copy in copies:
            copy.wait_recv()

    kinds = species[...]
    start = jnp.transpose(feats[...])
    mass = jnp.zeros((1, atoms), F32)
    for e in range(embed.shape[0]):
        column = jnp.transpose(jnp.broadcast_to(embed[e : e + 1, :], (128, channels)))
        column = jnp.concatenate([column] * (atoms // 128), axis=1)
        start = start + jnp.where(kinds == e, column, 0.0)
        mass = jnp.where(kinds == e, MASSES[e], mass)
    h0[...] = start
    hi, lo = split(start)
    wv0_t = jnp.transpose(w_value[0].astype(F32)).astype(BF16)
    values_zero = (dot(wv0_t, hi) + dot(wv0_t, lo)).astype(BF16)

    pos[...] = jnp.zeros_like(pos)
    for b in range(beads):
        for c in range(3):
            pos[b, c : c + 1, :] = coords[c, b : b + 1, :]
    atom_rows = lax.broadcasted_iota(jnp.int32, (atoms, 2 * ghosts), 0)
    for b in range(beads):
        handed[b] = jnp.where(ghost_rows[b : b + 1, :] == atom_rows, 1.0, 0.0).astype(BF16)
        hi, lo = split(pos[b])
        table = jnp.concatenate([values_zero, hi, lo], axis=0)
        text[b, :, :atoms] = table
        picked = dot(table, handed[b]).astype(BF16)
        halo0_out[b, 0] = picked[:, :ghosts]
        halo0_out[b, 1] = picked[:, ghosts:]

    pl.semaphore_wait(barrier, 2 + n_bead - 1)
    halo0 = [both_sides(0, b, halo0_out, halo0_in) for b in range(beads)]
    start_all(halo0[0])
    start_all(halo0[1])

    ext_rows = lax.broadcasted_iota(jnp.int32, (2 * atoms, atoms), 0)
    for b in range(beads):
        for s in range(slots):
            row = nbr[b, s : s + 1, :]
            sel[b, :, s * atoms : (s + 1) * atoms] = jnp.where(ext_rows == row, 1.0, 0.0).astype(BF16)

    def filter_rows(layer):
        hi, lo = split(jnp.transpose(w_filter[layer]))
        return jnp.concatenate([hi, hi, lo], axis=1)

    def transposed(weight):
        return jnp.transpose(weight.astype(F32)).astype(BF16)

    wf = [filter_rows(0), filter_rows(1)]
    wv1_t = transposed(w_value[1])
    wo_t = [transposed(w_out[0]), transposed(w_out[1])]
    read = jnp.transpose(jnp.broadcast_to(readout[...], (128, channels)))
    read = jnp.concatenate([read] * (atoms // 128), axis=1)
    state[0] = jnp.zeros(state.shape[1:], F32)
    for b in range(beads):
        for c in range(3):
            state[0, 0, b, c : c + 1, :] = coords[c, b : b + 1, :]
            state[0, 1, b, c : c + 1, :] = momenta[c, b : b + 1, :]

    centers = SPACING * lax.broadcasted_iota(jnp.int32, (16, atoms), 0).astype(F32)
    lanes = [slice(s * atoms, (s + 1) * atoms) for s in range(slots)]
    chunks = [slice(g * wide, (g + 1) * wide) for g in range(groups)]

    def slope(x, gate):
        return gate * (1.0 + x * (1.0 - gate))

    def layer_zero(b):
        text[b, :, atoms : atoms + ghosts] = halo0_in[b, 0]
        text[b, :, atoms + ghosts :] = halo0_in[b, 1]
        acc = jnp.zeros((channels, atoms), F32)
        for g in range(groups):
            got = dot(text[b], sel[b, :, chunks[g]])
            gv[b, :, chunks[g]] = got[:channels]
            for s in range(GROUP):
                here, there = lanes[g * GROUP + s], lanes[s]
                off = got[channels : channels + 8, there] + got[channels + 8 :, there] - pos[b]
                offs[b, 0:8, here] = off
                square = jnp.sum(off * off, axis=0, keepdims=True) + SOFTEN
                inverse = lax.rsqrt(square)
                offs[b, 8:16, here] = jnp.broadcast_to(inverse, (8, atoms))
                t = square * inverse - centers
                rad = jnp.exp(-WIDTH * (t * t))
                rads[b, 0, :, here] = stacked(rad)
                rads[b, 1, :, here] = stacked((-2.0 * WIDTH) * (t * rad))
                acc = acc + dot(wf[0], rads[b, 0, :, here]) * gv[b, :, here]
        update = dot(wo_t[0], acc.astype(BF16))
        u0[b] = update
        hidden = h0[...] + update * jax.nn.sigmoid(update)
        h1[b] = hidden
        value = dot(wv1_t, hidden.astype(BF16)).astype(BF16)
        v1[b] = value
        picked = dot(value, handed[b]).astype(BF16)
        halo1_out[b, 0] = picked[:, :ghosts]
        halo1_out[b, 1] = picked[:, ghosts:]
        copies = both_sides(1, b, halo1_out, halo1_in)
        start_all(copies)
        return copies

    def between(b):
        for g in range(groups):
            g1[b, :, chunks[g]] = dot(v1[b], sel[b, :atoms, chunks[g]])
        for here in lanes:
            p0[b, :, here] = dot(wf[0], rads[b, 1, :, here]) * gv[b, :, here]
            f1[b, :, here] = dot(wf[1], rads[b, 0, :, here])
            f1d[b, :, here] = dot(wf[1], rads[b, 1, :, here])

    def layer_one(b):
        far = jnp.concatenate([halo1_in[b, 0], halo1_in[b, 1]], axis=1)
        acc = jnp.zeros((channels, atoms), F32)
        for g in range(groups):
            got = dot(far, sel[b, atoms:, chunks[g]])
            for s in range(GROUP):
                here, there = lanes[g * GROUP + s], lanes[s]
                value = g1[b, :, here] + got[:, there]
                acc = acc + f1[b, :, here] * value
                g1[b, :, here] = f1d[b, :, here] * value
        update = dot(wo_t[1], acc.astype(BF16))
        gate = jax.nn.sigmoid(update)
        hidden = h1[b] + update * gate
        grad = read * slope(hidden, jax.nn.sigmoid(hidden))
        dh[b] = grad
        grad = grad * slope(update, gate)
        dms[b] = dot(w_out[1], grad.astype(BF16))
        total = jnp.zeros((channels, 2 * ghosts), F32)
        for g in range(groups):
            for s in range(GROUP):
                here = lanes[g * GROUP + s]
                back[b, :, here] = (f1[b, :, here] * dms[b]).astype(BF16)
            total = total + dot_nt(back[b, :, chunks[g]], sel[b, atoms:, chunks[g]])
        value = total.astype(BF16)
        grad_out[b, 0] = value[:, :ghosts]
        grad_out[b, 1] = value[:, ghosts:]
        copies = both_sides(2, b, grad_out, grad_in)
        start_all(copies)
        return copies

    def own_scatter(b):
        total = jnp.zeros((channels, atoms), F32)
        for g in range(groups):
            total = total + dot_nt(back[b, :, chunks[g]], sel[b, :atoms, chunks[g]])
        dv[b] = total
        for here in lanes:
            drs[b, :, here] = jnp.sum(dms[b] * g1[b, :, here], axis=0, keepdims=True)

    def backward(b):
        arrived = jnp.concatenate([grad_in[b, 0], grad_in[b, 1]], axis=1)
        value = dv[b] + dot_nt(arrived, handed[b])
        grad = dh[b] + dot(w_value[1], value.astype(BF16))
        update = u0[b]
        grad = grad * slope(update, jax.nn.sigmoid(update))
        message = dot(w_out[0], grad.astype(BF16))
        acc = jnp.zeros((8, atoms), F32)
        total = jnp.zeros((16, 2 * ghosts), F32)
        for g in range(groups):
            for s in range(GROUP):
                here = lanes[g * GROUP + s]
                slot = drs[b, :, here] + jnp.sum(message * p0[b, :, here], axis=0, keepdims=True)
                part = offs[b, 0:8, here] * offs[b, 8:16, here] * slot
                acc = acc + part
                parts[b, :, here] = jnp.concatenate(split(part), axis=0)
            total = total + dot_nt(parts[b, :, chunks[g]], sel[b, atoms:, chunks[g]])
        total = total[0:8] + total[8:16]
        pgrad_out[b, 0] = total[:, :ghosts]
        pgrad_out[b, 1] = total[:, ghosts:]
        copies = both_sides(3, b, pgrad_out, pgrad_in)
        start_all(copies)
        total = jnp.zeros((16, atoms), F32)
        for g in range(groups):
            total = total + dot_nt(parts[b, :, chunks[g]], sel[b, :atoms, chunks[g]])
        fown[b] = total[0:8] + total[8:16] - acc
        return copies

    def kick(b):
        arrived = jnp.concatenate([pgrad_in[b, 0], pgrad_in[b, 1]], axis=1)
        placed = dot_nt(jnp.concatenate(split(arrived), axis=0), handed[b])
        force[0, b] = ((-0.5 * STEP_DT) * (fown[b] + placed[0:8] + placed[8:16]))[0:4]
        copies = to_beads(force, lambda ref, o: ref.at[o, b], force_send.at[b], force_recv.at[b])
        start_all(copies)
        return copies

    arrive(halo0[0])
    halo1_0 = layer_zero(0)
    arrive(halo0[1])
    states = to_beads(state, lambda ref, o: ref.at[o], state_send, state_recv)
    start_all(states)
    halo1_1 = layer_zero(1)
    between(0)
    arrive(halo1_0)
    grads_0 = layer_one(0)
    between(1)
    arrive(halo1_1)
    grads_1 = layer_one(1)
    own_scatter(0)
    arrive(grads_0)
    pgrads_0 = backward(0)
    own_scatter(1)
    arrive(pgrads_0)
    forces_0 = kick(0)
    arrive(grads_1)
    pgrads_1 = backward(1)

    keep, drift, spring = ring_tables(beads * n_bead)

    def spread(table, sources):
        result = []
        for b in range(beads):
            total = jnp.zeros((4, atoms), F32)
            for o, pair in enumerate(sources):
                for c, source in enumerate(pair):
                    total = total + table[(beads * o + b - c) % len(table)] * source
            result.append(total)
        return result

    arrive(states)
    q_all = [[state[o, 0, c] for c in range(beads)] for o in range(n_bead)]
    p_all = [[state[o, 1, c] for c in range(beads)] for o in range(n_bead)]
    q_next = [x + y / mass for x, y in zip(spread(keep, q_all), spread(drift, p_all))]
    p_next = [x - mass * y for x, y in zip(spread(keep, p_all), spread(spring, q_all))]

    arrive(pgrads_1)
    forces_1 = kick(1)
    arrive(forces_0)
    arrive(forces_1)
    kicks = [[force[o, c] for c in range(beads)] for o in range(n_bead)]
    q_next = [x + y / mass for x, y in zip(q_next, spread(drift, kicks))]
    p_next = [x + y for x, y in zip(p_next, spread(keep, kicks))]
    for b in range(beads):
        for c in range(3):
            out_q[c, b : b + 1, :] = q_next[b][c : c + 1, :]
            out_p[c, b : b + 1, :] = p_next[b][c : c + 1, :]
    for copies in halo0 + [halo1_0, halo1_1, grads_0, grads_1, pgrads_0, pgrads_1, states, forces_0, forces_1]:
        for copy in copies:
            copy.wait_send()


def local(
    coords,
    momenta,
    species,
    atom_features,
    neighbours,
    ghost_rows,
    embed,
    w_filter,
    w_value,
    w_out,
    readout,
):
    n_bead, n_space = lax.axis_size("bead"), lax.axis_size("space")
    beads, _, atoms = coords.shape
    slots = neighbours.shape[2]
    ghosts = ghost_rows.shape[1] // 2
    channels = embed.shape[1]
    edges = slots * atoms
    rows = channels + 16
    vmem = pl.BlockSpec(memory_space=pltpu.VMEM)
    big = pltpu.VMEM((beads, channels, edges), F32)
    per_bead = pltpu.VMEM((beads, channels, atoms), F32)
    shape = jax.ShapeDtypeStruct((3, beads, atoms), F32)
    q_next, p_next = pl.pallas_call(
        functools.partial(kernel, n_bead, n_space),
        out_shape=(shape, shape),
        in_specs=[vmem] * 11,
        out_specs=(vmem, vmem),
        scratch_shapes=[
            pltpu.VMEM((beads, 2 * atoms, edges), BF16),
            pltpu.VMEM((beads, atoms, 2 * ghosts), BF16),
            pltpu.VMEM((beads, 8, atoms), F32),
            pltpu.VMEM((beads, rows, 2 * atoms), BF16),
            pltpu.VMEM((beads, 2, rows, ghosts), BF16),
            pltpu.VMEM((beads, 2, rows, ghosts), BF16),
            pltpu.VMEM((beads, 2, channels, ghosts), BF16),
            pltpu.VMEM((beads, 2, channels, ghosts), BF16),
            pltpu.VMEM((beads, 2, channels, ghosts), BF16),
            pltpu.VMEM((beads, 2, channels, ghosts), BF16),
            pltpu.VMEM((beads, 2, 8, ghosts), F32),
            pltpu.VMEM((beads, 2, 8, ghosts), F32),
            pltpu.VMEM((n_bead, 2, beads, 4, atoms), F32),
            pltpu.VMEM((n_bead, beads, 4, atoms), F32),
            pltpu.VMEM((beads, 16, edges), F32),
            pltpu.VMEM((beads, 2, 48, edges), BF16),
            big,
            big,
            big,
            big,
            big,
            pltpu.VMEM((channels, atoms), F32),
            per_bead,
            per_bead,
            pltpu.VMEM((beads, channels, atoms), BF16),
            pltpu.VMEM((beads, channels, edges), BF16),
            pltpu.VMEM((beads, 16, edges), BF16),
            per_bead,
            per_bead,
            pltpu.VMEM((beads, 1, edges), F32),
            per_bead,
            pltpu.VMEM((beads, 8, atoms), F32),
            pltpu.SemaphoreType.DMA((4, beads, 2)),
            pltpu.SemaphoreType.DMA((4, beads, 2)),
            pltpu.SemaphoreType.DMA((n_bead,)),
            pltpu.SemaphoreType.DMA((n_bead,)),
            pltpu.SemaphoreType.DMA((beads, n_bead)),
            pltpu.SemaphoreType.DMA((beads, n_bead)),
        ],
        compiler_params=pltpu.CompilerParams(
            collective_id=0, has_side_effects=True, vmem_limit_bytes=58 * 1024 * 1024
        ),
    )(
        jnp.transpose(coords, (1, 0, 2)),
        jnp.transpose(momenta, (1, 0, 2)),
        species.reshape(1, atoms),
        atom_features,
        jnp.transpose(neighbours, (0, 2, 1)),
        ghost_rows,
        embed,
        w_filter,
        w_value,
        w_out,
        readout.reshape(1, channels),
    )
    return jnp.transpose(q_next, (1, 0, 2)), jnp.transpose(p_next, (1, 0, 2))


def solution(mesh):
    placed = (
        P("bead", None, "space"),
        P("bead", None, "space"),
        P("space"),
        P("space", None),
        P("bead", "space", None),
        P("bead", "space"),
        P(),
        P(),
        P(),
        P(),
        P(),
    )
    return jax.shard_map(
        local,
        mesh=mesh,
        in_specs=placed,
        out_specs=(P("bead", None, "space"), P("bead", None, "space")),
        check_vma=False,
    )
```

time: 49.7 us -> 47.7 us (0.960)
  Pallas kernels: 46.6 us -> 44.2 us
    pallas_call x1, Pallas kernels: 46.6 us -> 44.2 us  [local(): pl.pallas_call(functools.partial(kernel, n_bead, n_space), out_shape=(sha...]
where the time goes in v2:
time: 47.7 us; the launch traced here: 46.9 us
  Pallas kernels  44.2 us (93%)
  local copies, waits for them, and re-layouts  1.97 us (4%)
  between operations  0.65 us (1%)
    pallas_call x1, Pallas kernels, local(): pl.pallas_call(functools.partial(kernel, n_bead, n_space), out_shape=(sha...  44.2 us
    unnamed x6, local copies, waits for them, and re-layouts  1.97 us

profile of v2, /device:TPU:32, one launch (start us, length us, event | category | flops | bytes accessed | tf_op | source)
XLA Modules:
  0.0 46.9 jit_solution(11052604812363980428)
XLA Ops:
  0.6 44.2 %shard_map.122 = (f32[3,2,256]{2,1,0:T(2,128)}, f32[3,2,256]{2,1,0:T(2,128)}) custom-call(f32[3,2,256]{2,1,0:T(2,128)} %bitcast.10, f32[3,2,256]{2,1,0:T(2,128)} %bitcast.11, s32[1,256]{1,0:T(1,128)} %bitcast.12, f32[256,128]{1,0:T(8,128)} %feats.1, s32[2,16,256]{2,1,0:T(8,128)} %bitcast.7, s32[2,256]{1,0:T(2,128)} %ghost_rows.1, f32[5,128]{1,0:T(8,128)} %embed.1, ...), custom_call_target="tpu_custom_call" | custom-call | tf_op jit(solution)/shard_map/pallas_call | solution.py:420
  44.9 0.0 copy-start.1
  44.9 0.7 %copy-done.1 = f32[3,2,256]{2,1,0:T(2,128)S(1)} copy-done((f32[3,2,256]{2,1,0:T(2,128)S(1)}, f32[3,2,256]{2,1,0:T(2,128)}, u32[]{:S(2)}) %copy-start.1) | copy-done | bytes 6168
  45.6 0.0 copy-start
  45.6 0.6 %copy.15 = f32[2,3,256]{2,0,1:T(2,128)} copy(f32[2,3,256]{2,0,1:T(2,128)S(1)} %bitcast.9) | data formatting | bytes 12288
  46.2 0.1 copy-done
  46.3 0.6 %copy.16 = f32[2,3,256]{2,0,1:T(2,128)} copy(f32[2,3,256]{2,0,1:T(2,128)S(1)} %bitcast.8) | data formatting | bytes 12288
Async XLA Ops:
  44.9 0.7 %copy-start.1 = (f32[3,2,256]{2,1,0:T(2,128)S(1)}, f32[3,2,256]{2,1,0:T(2,128)}, u32[]{:S(2)}) copy-start(f32[3,2,256]{2,1,0:T(2,128)} %get-tuple-element.4) | copy-start | bytes 18436
  45.6 0.7 %copy-start = (f32[3,2,256]{2,1,0:T(2,128)S(1)}, f32[3,2,256]{2,1,0:T(2,128)}, u32[]{:S(2)}) copy-start(f32[3,2,256]{2,1,0:T(2,128)} %get-tuple-element.5) | copy-start | bytes 18436

commit v3 on v2

--- a/solution.py
+++ b/solution.py
@@ -25,8 +25,9 @@
     return jnp.dot(a, b, preferred_element_type=F32)
 
 
-def dot_nt(a, b):
-    return lax.dot_general(a, b, (((1,), (1,)), ((), ())), preferred_element_type=F32)
+def one_hot(index, places):
+    index = jnp.broadcast_to(index, places.shape)
+    return jnp.where(index == places, jnp.ones(places.shape, BF16), jnp.zeros(places.shape, BF16))
 
 
 def split(x):
@@ -71,7 +72,9 @@
     out_q,
     out_p,
     sel,
+    sel_t,
     handed,
+    given,
     pos,
     text,
     halo0_out,
@@ -83,13 +86,13 @@
     pgrad_out,
     pgrad_in,
     state,
-    force,
+    kicked,
+    momentum,
     offs,
     rads,
     gv,
     p0,
     f1,
-    f1d,
     g1,
     h0,
     h1,
@@ -106,8 +109,9 @@
     halo_recv,
     state_send,
     state_recv,
-    force_send,
-    force_recv,
+    kick_send,
+    kick_recv,
+    ready,
 ):
     beads, atoms = 2, coords.shape[2]
     ghosts = ghost_rows.shape[1] // 2
@@ -120,14 +124,21 @@
     left = lax.rem(me_s + n_space - 1, n_space)
     right = lax.rem(me_s + 1, n_space)
 
+    def signal(semaphore, offsets):
+        for o in offsets:
+            peer = lax.rem(me_b + (o % n_bead), n_bead)
+            pl.semaphore_signal(semaphore, inc=1, device_id={"bead": peer}, device_id_type=MESH)
+
+    near, far_out = (1, -1, 8), (2, -2, 8)
     barrier = pltpu.get_barrier_semaphore()
     for side in (left, right):
         pl.semaphore_signal(barrier, inc=1, device_id={"space": side}, device_id_type=MESH)
-    for o in range(1, n_bead):
-        peer = lax.rem(me_b + o, n_bead)
-        pl.semaphore_signal(barrier, inc=1, device_id={"bead": peer}, device_id_type=MESH)
-
-    def both_sides(number, b, src, dst):
+    signal(barrier, near)
+
+    halos = ((halo0_out, halo0_in), (halo1_out, halo1_in), (grad_out, grad_in), (pgrad_out, pgrad_in))
+
+    def halo(number, b):
+        src, dst = halos[number]
         return [
             pltpu.make_async_remote_copy(
                 src_ref=src.at[b, mine],
@@ -140,11 +151,11 @@
             for mine, side in enumerate((left, right))
         ]
 
-    def to_beads(buffer, part, send, recv):
+    def to_beads(source, part, send, recv):
         return [
             pltpu.make_async_remote_copy(
-                src_ref=part(buffer, 0),
-                dst_ref=part(buffer, o),
+                src_ref=source,
+                dst_ref=part(o),
                 send_sem=send.at[o],
                 recv_sem=recv.at[o],
                 device_id={"bead": lax.rem(me_b + o, n_bead)},
@@ -152,6 +163,12 @@
             )
             for o in range(1, n_bead)
         ]
+
+    def states():
+        return to_beads(coords, lambda o: state.at[o], state_send, state_recv)
+
+    def kicks(b):
+        return to_beads(kicked.at[0, b], lambda o: kicked.at[o, b], kick_send.at[b], kick_recv.at[b])
 
     def start_all(copies):
         for copy in copies:
@@ -178,26 +195,41 @@
     for b in range(beads):
         for c in range(3):
             pos[b, c : c + 1, :] = coords[c, b : b + 1, :]
-    atom_rows = lax.broadcasted_iota(jnp.int32, (atoms, 2 * ghosts), 0)
-    for b in range(beads):
-        handed[b] = jnp.where(ghost_rows[b : b + 1, :] == atom_rows, 1.0, 0.0).astype(BF16)
+    atom_rows = lax.broadcasted_iota(jnp.int32, (atoms, atoms), 0).astype(F32).astype(BF16)
+    atom_lanes = lax.broadcasted_iota(jnp.int32, (atoms, atoms), 1).astype(F32).astype(BF16)
+    for b in range(beads):
+        handed[b] = one_hot(ghost_rows[b : b + 1, :].astype(F32).astype(BF16), atom_rows)
         hi, lo = split(pos[b])
         table = jnp.concatenate([values_zero, hi, lo], axis=0)
-        text[b, :, :atoms] = table
+        text[b] = table
         picked = dot(table, handed[b]).astype(BF16)
         halo0_out[b, 0] = picked[:, :ghosts]
         halo0_out[b, 1] = picked[:, ghosts:]
 
-    pl.semaphore_wait(barrier, 2 + n_bead - 1)
-    halo0 = [both_sides(0, b, halo0_out, halo0_in) for b in range(beads)]
-    start_all(halo0[0])
-    start_all(halo0[1])
-
-    ext_rows = lax.broadcasted_iota(jnp.int32, (2 * atoms, atoms), 0)
-    for b in range(beads):
+    pl.semaphore_wait(barrier, 2 + len(near))
+    for b in range(beads):
+        start_all(halo(0, b))
+    signal(ready.at[0], near)
+
+    for b in range(beads):
+        lists = nbr[b].astype(F32)
+        halves = [lists.astype(BF16), (lists - float(atoms)).astype(BF16)]
         for s in range(slots):
-            row = nbr[b, s : s + 1, :]
-            sel[b, :, s * atoms : (s + 1) * atoms] = jnp.where(ext_rows == row, 1.0, 0.0).astype(BF16)
+            here = slice(s * atoms, (s + 1) * atoms)
+            for half, value in enumerate(halves):
+                sel[b, half * atoms : (half + 1) * atoms, here] = one_hot(value[s : s + 1, :], atom_rows)
+        got = dot(text[b], sel[b, :atoms, :])
+        gv[b] = got[:channels]
+        offs[b] = got[channels:]
+    for b in range(beads):
+        marks = jnp.broadcast_to(ghost_rows[b : b + 1, :], (8, 2 * ghosts))
+        columns = jnp.transpose(jnp.concatenate([nbr[b], marks], axis=0)).astype(F32)
+        given[b] = one_hot(columns[:, slots : slots + 1].astype(BF16), atom_lanes)
+        for s in range(slots):
+            here = slice(s * atoms, (s + 1) * atoms)
+            column = jnp.broadcast_to(columns[:, s : s + 1], (atoms, atoms))
+            sel_t[b, here, :atoms] = one_hot(column.astype(BF16), atom_lanes)
+            sel_t[b, here, atoms:] = one_hot((column - float(atoms)).astype(BF16), atom_lanes)
 
     def filter_rows(layer):
         hi, lo = split(jnp.transpose(w_filter[layer]))
@@ -211,11 +243,10 @@
     wo_t = [transposed(w_out[0]), transposed(w_out[1])]
     read = jnp.transpose(jnp.broadcast_to(readout[...], (128, channels)))
     read = jnp.concatenate([read] * (atoms // 128), axis=1)
-    state[0] = jnp.zeros(state.shape[1:], F32)
+    momentum[...] = jnp.zeros_like(momentum)
     for b in range(beads):
         for c in range(3):
-            state[0, 0, b, c : c + 1, :] = coords[c, b : b + 1, :]
-            state[0, 1, b, c : c + 1, :] = momenta[c, b : b + 1, :]
+            momentum[b, c : c + 1, :] = momenta[c, b : b + 1, :]
 
     centers = SPACING * lax.broadcasted_iota(jnp.int32, (16, atoms), 0).astype(F32)
     lanes = [slice(s * atoms, (s + 1) * atoms) for s in range(slots)]
@@ -225,15 +256,14 @@
         return gate * (1.0 + x * (1.0 - gate))
 
     def layer_zero(b):
-        text[b, :, atoms : atoms + ghosts] = halo0_in[b, 0]
-        text[b, :, atoms + ghosts :] = halo0_in[b, 1]
+        far = jnp.concatenate([halo0_in[b, 0], halo0_in[b, 1]], axis=1)
         acc = jnp.zeros((channels, atoms), F32)
         for g in range(groups):
-            got = dot(text[b], sel[b, :, chunks[g]])
-            gv[b, :, chunks[g]] = got[:channels]
+            got = dot(far, sel[b, atoms:, chunks[g]])
             for s in range(GROUP):
                 here, there = lanes[g * GROUP + s], lanes[s]
-                off = got[channels : channels + 8, there] + got[channels + 8 :, there] - pos[b]
+                place = got[channels:, there] + offs[b, :, here]
+                off = place[0:8] + place[8:16] - pos[b]
                 offs[b, 0:8, here] = off
                 square = jnp.sum(off * off, axis=0, keepdims=True) + SOFTEN
                 inverse = lax.rsqrt(square)
@@ -242,7 +272,9 @@
                 rad = jnp.exp(-WIDTH * (t * t))
                 rads[b, 0, :, here] = stacked(rad)
                 rads[b, 1, :, here] = stacked((-2.0 * WIDTH) * (t * rad))
-                acc = acc + dot(wf[0], rads[b, 0, :, here]) * gv[b, :, here]
+                value = got[:channels, there] + gv[b, :, here]
+                gv[b, :, here] = value
+                acc = acc + dot(wf[0], rads[b, 0, :, here]) * value
         update = dot(wo_t[0], acc.astype(BF16))
         u0[b] = update
         hidden = h0[...] + update * jax.nn.sigmoid(update)
@@ -252,17 +284,13 @@
         picked = dot(value, handed[b]).astype(BF16)
         halo1_out[b, 0] = picked[:, :ghosts]
         halo1_out[b, 1] = picked[:, ghosts:]
-        copies = both_sides(1, b, halo1_out, halo1_in)
-        start_all(copies)
-        return copies
+        start_all(halo(1, b))
 
     def between(b):
         for g in range(groups):
             g1[b, :, chunks[g]] = dot(v1[b], sel[b, :atoms, chunks[g]])
         for here in lanes:
-            p0[b, :, here] = dot(wf[0], rads[b, 1, :, here]) * gv[b, :, here]
             f1[b, :, here] = dot(wf[1], rads[b, 0, :, here])
-            f1d[b, :, here] = dot(wf[1], rads[b, 1, :, here])
 
     def layer_one(b):
         far = jnp.concatenate([halo1_in[b, 0], halo1_in[b, 1]], axis=1)
@@ -273,7 +301,7 @@
                 here, there = lanes[g * GROUP + s], lanes[s]
                 value = g1[b, :, here] + got[:, there]
                 acc = acc + f1[b, :, here] * value
-                g1[b, :, here] = f1d[b, :, here] * value
+                g1[b, :, here] = value
         update = dot(wo_t[1], acc.astype(BF16))
         gate = jax.nn.sigmoid(update)
         hidden = h1[b] + update * gate
@@ -286,25 +314,25 @@
             for s in range(GROUP):
                 here = lanes[g * GROUP + s]
                 back[b, :, here] = (f1[b, :, here] * dms[b]).astype(BF16)
-            total = total + dot_nt(back[b, :, chunks[g]], sel[b, atoms:, chunks[g]])
+            total = total + dot(back[b, :, chunks[g]], sel_t[b, chunks[g], atoms:])
         value = total.astype(BF16)
         grad_out[b, 0] = value[:, :ghosts]
         grad_out[b, 1] = value[:, ghosts:]
-        copies = both_sides(2, b, grad_out, grad_in)
-        start_all(copies)
-        return copies
+        start_all(halo(2, b))
 
     def own_scatter(b):
         total = jnp.zeros((channels, atoms), F32)
         for g in range(groups):
-            total = total + dot_nt(back[b, :, chunks[g]], sel[b, :atoms, chunks[g]])
+            total = total + dot(back[b, :, chunks[g]], sel_t[b, chunks[g], :atoms])
         dv[b] = total
         for here in lanes:
-            drs[b, :, here] = jnp.sum(dms[b] * g1[b, :, here], axis=0, keepdims=True)
+            p0[b, :, here] = dot(wf[0], rads[b, 1, :, here]) * gv[b, :, here]
+            change = dot(wf[1], rads[b, 1, :, here]) * g1[b, :, here]
+            drs[b, :, here] = jnp.sum(dms[b] * change, axis=0, keepdims=True)
 
     def backward(b):
         arrived = jnp.concatenate([grad_in[b, 0], grad_in[b, 1]], axis=1)
-        value = dv[b] + dot_nt(arrived, handed[b])
+        value = dv[b] + dot(arrived, given[b])
         grad = dh[b] + dot(w_value[1], value.astype(BF16))
         update = u0[b]
         grad = grad * slope(update, jax.nn.sigmoid(update))
@@ -318,77 +346,82 @@
                 part = offs[b, 0:8, here] * offs[b, 8:16, here] * slot
                 acc = acc + part
                 parts[b, :, here] = jnp.concatenate(split(part), axis=0)
-            total = total + dot_nt(parts[b, :, chunks[g]], sel[b, atoms:, chunks[g]])
+            total = total + dot(parts[b, :, chunks[g]], sel_t[b, chunks[g], atoms:])
         total = total[0:8] + total[8:16]
         pgrad_out[b, 0] = total[:, :ghosts]
         pgrad_out[b, 1] = total[:, ghosts:]
-        copies = both_sides(3, b, pgrad_out, pgrad_in)
-        start_all(copies)
+        start_all(halo(3, b))
         total = jnp.zeros((16, atoms), F32)
         for g in range(groups):
-            total = total + dot_nt(parts[b, :, chunks[g]], sel[b, :atoms, chunks[g]])
+            total = total + dot(parts[b, :, chunks[g]], sel_t[b, chunks[g], :atoms])
         fown[b] = total[0:8] + total[8:16] - acc
-        return copies
 
     def kick(b):
         arrived = jnp.concatenate([pgrad_in[b, 0], pgrad_in[b, 1]], axis=1)
-        placed = dot_nt(jnp.concatenate(split(arrived), axis=0), handed[b])
-        force[0, b] = ((-0.5 * STEP_DT) * (fown[b] + placed[0:8] + placed[8:16]))[0:4]
-        copies = to_beads(force, lambda ref, o: ref.at[o, b], force_send.at[b], force_recv.at[b])
-        start_all(copies)
-        return copies
-
-    arrive(halo0[0])
-    halo1_0 = layer_zero(0)
-    arrive(halo0[1])
-    states = to_beads(state, lambda ref, o: ref.at[o], state_send, state_recv)
-    start_all(states)
-    halo1_1 = layer_zero(1)
+        placed = dot(jnp.concatenate(split(arrived), axis=0), given[b])
+        grad = fown[b] + placed[0:8] + placed[8:16]
+        kicked[0, b] = momentum[b] - (0.5 * STEP_DT) * grad[0:4]
+        start_all(kicks(b))
+
+    arrive(halo(0, 0))
+    arrive(halo(0, 1))
+    pl.semaphore_wait(ready.at[0], len(near))
+    signal(ready.at[1], far_out)
+    layer_zero(0)
+    layer_zero(1)
     between(0)
-    arrive(halo1_0)
-    grads_0 = layer_one(0)
+    pl.semaphore_wait(ready.at[1], len(far_out))
+    start_all(states())
     between(1)
-    arrive(halo1_1)
-    grads_1 = layer_one(1)
+    arrive(halo(1, 0))
+    layer_one(0)
+    arrive(halo(1, 1))
+    layer_one(1)
     own_scatter(0)
-    arrive(grads_0)
-    pgrads_0 = backward(0)
     own_scatter(1)
-    arrive(pgrads_0)
-    forces_0 = kick(0)
-    arrive(grads_1)
-    pgrads_1 = backward(1)
+    arrive(halo(2, 0))
+    backward(0)
+    arrive(halo(2, 1))
+    backward(1)
 
     keep, drift, spring = ring_tables(beads * n_bead)
 
-    def spread(table, sources):
-        result = []
+    def of_positions(table):
+        same = jnp.zeros((3, beads, atoms), F32)
+        other = jnp.zeros((3, beads, atoms), F32)
+        first = lax.broadcasted_iota(jnp.int32, (3, beads, atoms), 1) == 0
+        count = len(table)
+        for o in range(n_bead):
+            source = coords[...] if o == 0 else state[o]
+            same = same + table[(2 * o) % count] * source
+            other = other + jnp.where(first, table[(2 * o + 1) % count], table[(2 * o - 1) % count]) * source
+        return same + jnp.concatenate([other[:, 1:], other[:, :1]], axis=1)
+
+    arrive(halo(3, 0))
+    kick(0)
+    arrive(states())
+    q_base = of_positions(keep)
+    p_base = of_positions(spring)
+    arrive(halo(3, 1))
+    kick(1)
+    q_next = [jnp.zeros((4, atoms), F32)] * beads
+    p_next = [jnp.zeros((4, atoms), F32)] * beads
+    for c in range(beads):
+        arrive(kicks(c))
         for b in range(beads):
-            total = jnp.zeros((4, atoms), F32)
-            for o, pair in enumerate(sources):
-                for c, source in enumerate(pair):
-                    total = total + table[(beads * o + b - c) % len(table)] * source
-            result.append(total)
-        return result
-
-    arrive(states)
-    q_all = [[state[o, 0, c] for c in range(beads)] for o in range(n_bead)]
-    p_all = [[state[o, 1, c] for c in range(beads)] for o in range(n_bead)]
-    q_next = [x + y / mass for x, y in zip(spread(keep, q_all), spread(drift, p_all))]
-    p_next = [x - mass * y for x, y in zip(spread(keep, p_all), spread(spring, q_all))]
-
-    arrive(pgrads_1)
-    forces_1 = kick(1)
-    arrive(forces_0)
-    arrive(forces_1)
-    kicks = [[force[o, c] for c in range(beads)] for o in range(n_bead)]
-    q_next = [x + y / mass for x, y in zip(q_next, spread(drift, kicks))]
-    p_next = [x + y for x, y in zip(p_next, spread(keep, kicks))]
-    for b in range(beads):
+            for o in range(n_bead):
+                apart = (beads * o + b - c) % len(keep)
+                source = kicked[o, c]
+                q_next[b] = q_next[b] + drift[apart] * source
+                p_next[b] = p_next[b] + keep[apart] * source
+    for b in range(beads):
+        q_next[b] = q_next[b] / mass
         for c in range(3):
-            out_q[c, b : b + 1, :] = q_next[b][c : c + 1, :]
-            out_p[c, b : b + 1, :] = p_next[b][c : c + 1, :]
-    for copies in halo0 + [halo1_0, halo1_1, grads_0, grads_1, pgrads_0, pgrads_1, states, forces_0, forces_1]:
+            out_q[c, b : b + 1, :] = q_base[c, b : b + 1] + q_next[b][c : c + 1, :]
+            out_p[c, b : b + 1, :] = p_next[b][c : c + 1, :] - mass * p_base[c, b : b + 1]
+    sent = [states()] + [kicks(b) for b in range(beads)]
+    sent += [halo(number, b) for number in range(len(halos)) for b in range(beads)]
+    for copies in sent:
         for copy in copies:
             copy.wait_send()
 
@@ -419,14 +452,16 @@
     shape = jax.ShapeDtypeStruct((3, beads, atoms), F32)
     q_next, p_next = pl.pallas_call(
         functools.partial(kernel, n_bead, n_space),
-        out_shape=(shape, shape),
+        out_shape=(pltpu.VMEM((3, beads, atoms), F32),) * 2,
         in_specs=[vmem] * 11,
         out_specs=(vmem, vmem),
         scratch_shapes=[
             pltpu.VMEM((beads, 2 * atoms, edges), BF16),
+            pltpu.VMEM((beads, edges, 2 * atoms), BF16),
             pltpu.VMEM((beads, atoms, 2 * ghosts), BF16),
+            pltpu.VMEM((beads, 2 * ghosts, atoms), BF16),
             pltpu.VMEM((beads, 8, atoms), F32),
-            pltpu.VMEM((beads, rows, 2 * atoms), BF16),
+            pltpu.VMEM((beads, rows, atoms), BF16),
             pltpu.VMEM((beads, 2, rows, ghosts), BF16),
             pltpu.VMEM((beads, 2, rows, ghosts), BF16),
             pltpu.VMEM((beads, 2, channels, ghosts), BF16),
@@ -435,11 +470,11 @@
             pltpu.VMEM((beads, 2, channels, ghosts), BF16),
             pltpu.VMEM((beads, 2, 8, ghosts), F32),
             pltpu.VMEM((beads, 2, 8, ghosts), F32),
-            pltpu.VMEM((n_bead, 2, beads, 4, atoms), F32),
+            pltpu.VMEM((n_bead, 3, beads, atoms), F32),
             pltpu.VMEM((n_bead, beads, 4, atoms), F32),
+            pltpu.VMEM((beads, 4, atoms), F32),
             pltpu.VMEM((beads, 16, edges), F32),
             pltpu.VMEM((beads, 2, 48, edges), BF16),
-            big,
             big,
             big,
             big,
@@ -461,6 +496,7 @@
             pltpu.SemaphoreType.DMA((n_bead,)),
             pltpu.SemaphoreType.DMA((beads, n_bead)),
             pltpu.SemaphoreType.DMA((beads, n_bead)),
+            pltpu.SemaphoreType.REGULAR((2,)),
         ],
         compiler_params=pltpu.CompilerParams(
             collective_id=0, has_side_effects=True, vmem_limit_bytes=58 * 1024 * 1024

time: 47.7 us -> 39 us (0.82); the launches traced: 46.9 us -> 38.9 us
  Pallas kernels: 44.2 us -> 37.1 us
  local copies, waits for them, and re-layouts: 1.97 us -> 1.19 us
    pallas_call x1, Pallas kernels: 44.2 us -> 37.1 us  [local(): pl.pallas_call(functools.partial(kernel, n_bead, n_space), out_shape=(plt...]
    unnamed x6 -> x2, local copies, waits for them, and re-layouts: 1.97 us -> 1.19 us
where the time goes in v3:
time: 39 us; the launch traced here: 38.9 us
  Pallas kernels  37.1 us (95%)
  local copies, waits for them, and re-layouts  1.19 us (3%)
  between operations  0.64 us (2%)
    pallas_call x1, Pallas kernels, local(): pl.pallas_call(functools.partial(kernel, n_bead, n_space), out_shape=(plt...  37.1 us
    unnamed x2, local copies, waits for them, and re-layouts  1.19 us

profile of v3, /device:TPU:32, one launch (start us, length us, event | category | flops | bytes accessed | tf_op | source)
XLA Modules:
  0.0 38.9 jit_solution(3896651177391287888)
XLA Ops:
  0.6 37.1 %shard_map.122 = (f32[3,2,256]{2,1,0:T(2,128)S(1)}, f32[3,2,256]{2,1,0:T(2,128)S(1)}) custom-call(f32[3,2,256]{2,1,0:T(2,128)} %bitcast.10, f32[3,2,256]{2,1,0:T(2,128)} %bitcast.11, s32[1,256]{1,0:T(1,128)} %bitcast.12, f32[256,128]{1,0:T(8,128)} %feats.1, s32[2,16,256]{2,1,0:T(8,128)} %bitcast.9, s32[2,256]{1,0:T(2,128)} %ghost_rows.1, f32[5,128]{1,0:T(8,128)} %embed.1, ...), custom_call_target="tpu_custom_call" | custom-call | tf_op jit(solution)/shard_map/pallas_call | solution.py:453
  37.7 0.6 %copy.15 = f32[2,3,256]{2,0,1:T(2,128)} copy(f32[2,3,256]{2,0,1:T(2,128)S(1)} %bitcast.8) | data formatting | bytes 12288
  38.3 0.6 %copy.16 = f32[2,3,256]{2,0,1:T(2,128)} copy(f32[2,3,256]{2,0,1:T(2,128)S(1)} %bitcast.7) | data formatting | bytes 12288

commit v4 on v3

--- a/solution.py
+++ b/solution.py
@@ -58,6 +58,18 @@
 def kernel(
     n_bead,
     n_space,
+    coords_hbm,
+    momenta_hbm,
+    species_hbm,
+    feats_hbm,
+    nbr_hbm,
+    ghost_rows_hbm,
+    embed_hbm,
+    w_filter_hbm,
+    w_value_hbm,
+    w_out_hbm,
+    readout_hbm,
+    out,
     coords,
     momenta,
     species,
@@ -69,8 +81,6 @@
     w_value,
     w_out,
     readout,
-    out_q,
-    out_p,
     sel,
     sel_t,
     handed,
@@ -90,9 +100,11 @@
     momentum,
     offs,
     rads,
+    apart,
     gv,
     p0,
     f1,
+    f1_short,
     g1,
     h0,
     h1,
@@ -112,8 +124,9 @@
     kick_send,
     kick_recv,
     ready,
+    fetch,
 ):
-    beads, atoms = 2, coords.shape[2]
+    beads, atoms = coords.shape[1:]
     ghosts = ghost_rows.shape[1] // 2
     channels = feats.shape[1]
     slots = nbr.shape[1]
@@ -129,11 +142,36 @@
             peer = lax.rem(me_b + (o % n_bead), n_bead)
             pl.semaphore_signal(semaphore, inc=1, device_id={"bead": peer}, device_id_type=MESH)
 
+    fetched = dict(
+        (name, pltpu.make_async_copy(source, here, fetch.at[i]))
+        for i, (name, source, here) in enumerate(
+            (
+                ("feats", feats_hbm, feats),
+                ("species", species_hbm, species),
+                ("embed", embed_hbm, embed),
+                ("w_value", w_value_hbm, w_value),
+                ("ghost_rows", ghost_rows_hbm, ghost_rows),
+                ("coords", coords_hbm, coords),
+                ("nbr", nbr_hbm, nbr),
+                ("w_filter", w_filter_hbm, w_filter),
+                ("w_out", w_out_hbm, w_out),
+                ("readout", readout_hbm, readout),
+                ("momenta", momenta_hbm, momenta),
+            )
+        )
+    )
+
+    def fetch_done(*names):
+        for name in names:
+            fetched[name].wait()
+
     near, far_out = (1, -1, 8), (2, -2, 8)
     barrier = pltpu.get_barrier_semaphore()
     for side in (left, right):
         pl.semaphore_signal(barrier, inc=1, device_id={"space": side}, device_id_type=MESH)
     signal(barrier, near)
+    for copy in fetched.values():
+        copy.start()
 
     halos = ((halo0_out, halo0_in), (halo1_out, halo1_in), (grad_out, grad_in), (pgrad_out, pgrad_in))
 
@@ -161,8 +199,11 @@
                 device_id={"bead": lax.rem(me_b + o, n_bead)},
                 device_id_type=MESH,
             )
-            for o in range(1, n_bead)
+            for o in outward
         ]
+
+    half = n_bead // 2
+    outward = sorted(range(1, n_bead), key=lambda o: -2 * min(o % half, half - o % half) - o // half)
 
     def states():
         return to_beads(coords, lambda o: state.at[o], state_send, state_recv)
@@ -178,6 +219,7 @@
         for copy in copies:
             copy.wait_recv()
 
+    fetch_done("feats", "species", "embed", "w_value", "ghost_rows", "coords")
     kinds = species[...]
     start = jnp.transpose(feats[...])
     mass = jnp.zeros((1, atoms), F32)
@@ -211,6 +253,7 @@
         start_all(halo(0, b))
     signal(ready.at[0], near)
 
+    fetch_done("nbr")
     for b in range(beads):
         lists = nbr[b].astype(F32)
         halves = [lists.astype(BF16), (lists - float(atoms)).astype(BF16)]
@@ -231,6 +274,7 @@
             sel_t[b, here, :atoms] = one_hot(column.astype(BF16), atom_lanes)
             sel_t[b, here, atoms:] = one_hot((column - float(atoms)).astype(BF16), atom_lanes)
 
+    fetch_done("w_filter", "w_out", "readout", "momenta")
     def filter_rows(layer):
         hi, lo = split(jnp.transpose(w_filter[layer]))
         return jnp.concatenate([hi, hi, lo], axis=1)
@@ -269,12 +313,11 @@
                 inverse = lax.rsqrt(square)
                 offs[b, 8:16, here] = jnp.broadcast_to(inverse, (8, atoms))
                 t = square * inverse - centers
-                rad = jnp.exp(-WIDTH * (t * t))
-                rads[b, 0, :, here] = stacked(rad)
-                rads[b, 1, :, here] = stacked((-2.0 * WIDTH) * (t * rad))
+                apart[b, :, here] = t
+                rads[b, :, here] = stacked(jnp.exp(-WIDTH * (t * t)))
                 value = got[:channels, there] + gv[b, :, here]
                 gv[b, :, here] = value
-                acc = acc + dot(wf[0], rads[b, 0, :, here]) * value
+                acc = acc + dot(wf[0], rads[b, :, here]) * value
         update = dot(wo_t[0], acc.astype(BF16))
         u0[b] = update
         hidden = h0[...] + update * jax.nn.sigmoid(update)
@@ -290,7 +333,9 @@
         for g in range(groups):
             g1[b, :, chunks[g]] = dot(v1[b], sel[b, :atoms, chunks[g]])
         for here in lanes:
-            f1[b, :, here] = dot(wf[1], rads[b, 0, :, here])
+            weight = dot(wf[1], rads[b, :, here])
+            f1[b, :, here] = weight
+            f1_short[b, :, here] = weight.astype(BF16)
 
     def layer_one(b):
         far = jnp.concatenate([halo1_in[b, 0], halo1_in[b, 1]], axis=1)
@@ -308,12 +353,14 @@
         grad = read * slope(hidden, jax.nn.sigmoid(hidden))
         dh[b] = grad
         grad = grad * slope(update, gate)
-        dms[b] = dot(w_out[1], grad.astype(BF16))
+        message = dot(w_out[1], grad.astype(BF16))
+        dms[b] = message
+        short = message.astype(BF16)
         total = jnp.zeros((channels, 2 * ghosts), F32)
         for g in range(groups):
             for s in range(GROUP):
                 here = lanes[g * GROUP + s]
-                back[b, :, here] = (f1[b, :, here] * dms[b]).astype(BF16)
+                back[b, :, here] = f1_short[b, :, here] * short
             total = total + dot(back[b, :, chunks[g]], sel_t[b, chunks[g], atoms:])
         value = total.astype(BF16)
         grad_out[b, 0] = value[:, :ghosts]
@@ -326,8 +373,10 @@
             total = total + dot(back[b, :, chunks[g]], sel_t[b, chunks[g], :atoms])
         dv[b] = total
         for here in lanes:
-            p0[b, :, here] = dot(wf[0], rads[b, 1, :, here]) * gv[b, :, here]
-            change = dot(wf[1], rads[b, 1, :, here]) * g1[b, :, here]
+            t = apart[b, :, here]
+            steep = stacked((-2.0 * WIDTH) * (t * jnp.exp(-WIDTH * (t * t))))
+            p0[b, :, here] = dot(wf[0], steep) * gv[b, :, here]
+            change = dot(wf[1], steep) * g1[b, :, here]
             drs[b, :, here] = jnp.sum(dms[b] * change, axis=0, keepdims=True)
 
     def backward(b):
@@ -402,23 +451,26 @@
     arrive(states())
     q_base = of_positions(keep)
     p_base = of_positions(spring)
+    inverse_mass = 1.0 / mass
     arrive(halo(3, 1))
     kick(1)
     q_next = [jnp.zeros((4, atoms), F32)] * beads
     p_next = [jnp.zeros((4, atoms), F32)] * beads
     for c in range(beads):
-        arrive(kicks(c))
-        for b in range(beads):
-            for o in range(n_bead):
-                apart = (beads * o + b - c) % len(keep)
-                source = kicked[o, c]
-                q_next[b] = q_next[b] + drift[apart] * source
-                p_next[b] = p_next[b] + keep[apart] * source
+        arrivals = kicks(c)
+        for o in [0] + outward[::-1]:
+            if o:
+                arrivals[outward.index(o)].wait_recv()
+            source = kicked[o, c]
+            for b in range(beads):
+                d = (beads * o + b - c) % len(keep)
+                q_next[b] = q_next[b] + drift[d] * source
+                p_next[b] = p_next[b] + keep[d] * source
     for b in range(beads):
-        q_next[b] = q_next[b] / mass
+        q_next[b] = q_next[b] * inverse_mass
         for c in range(3):
-            out_q[c, b : b + 1, :] = q_base[c, b : b + 1] + q_next[b][c : c + 1, :]
-            out_p[c, b : b + 1, :] = p_next[b][c : c + 1, :] - mass * p_base[c, b : b + 1]
+            out[0, c, b : b + 1, :] = q_base[c, b : b + 1] + q_next[b][c : c + 1, :]
+            out[1, c, b : b + 1, :] = p_next[b][c : c + 1, :] - mass * p_base[c, b : b + 1]
     sent = [states()] + [kicks(b) for b in range(beads)]
     sent += [halo(number, b) for number in range(len(halos)) for b in range(beads)]
     for copies in sent:
@@ -450,12 +502,23 @@
     big = pltpu.VMEM((beads, channels, edges), F32)
     per_bead = pltpu.VMEM((beads, channels, atoms), F32)
     shape = jax.ShapeDtypeStruct((3, beads, atoms), F32)
-    q_next, p_next = pl.pallas_call(
+    result = pl.pallas_call(
         functools.partial(kernel, n_bead, n_space),
-        out_shape=(pltpu.VMEM((3, beads, atoms), F32),) * 2,
-        in_specs=[vmem] * 11,
-        out_specs=(vmem, vmem),
+        out_shape=pltpu.VMEM((2, 3, beads, atoms), F32),
+        in_specs=[pl.BlockSpec(memory_space=pl.ANY)] * 11,
+        out_specs=vmem,
         scratch_shapes=[
+            pltpu.VMEM((3, beads, atoms), F32),
+            pltpu.VMEM((3, beads, atoms), F32),
+            pltpu.VMEM((1, atoms), jnp.int32),
+            pltpu.VMEM(atom_features.shape, F32),
+            pltpu.VMEM((beads, slots, atoms), jnp.int32),
+            pltpu.VMEM(ghost_rows.shape, jnp.int32),
+            pltpu.VMEM(embed.shape, F32),
+            pltpu.VMEM(w_filter.shape, F32),
+            pltpu.VMEM(w_value.shape, BF16),
+            pltpu.VMEM(w_out.shape, BF16),
+            pltpu.VMEM((1, channels), F32),
             pltpu.VMEM((beads, 2 * atoms, edges), BF16),
             pltpu.VMEM((beads, edges, 2 * atoms), BF16),
             pltpu.VMEM((beads, atoms, 2 * ghosts), BF16),
@@ -474,10 +537,12 @@
             pltpu.VMEM((n_bead, beads, 4, atoms), F32),
             pltpu.VMEM((beads, 4, atoms), F32),
             pltpu.VMEM((beads, 16, edges), F32),
-            pltpu.VMEM((beads, 2, 48, edges), BF16),
+            pltpu.VMEM((beads, 48, edges), BF16),
+            pltpu.VMEM((beads, 16, edges), F32),
             big,
             big,
             big,
+            pltpu.VMEM((beads, channels, edges), BF16),
             big,
             pltpu.VMEM((channels, atoms), F32),
             per_bead,
@@ -497,9 +562,10 @@
             pltpu.SemaphoreType.DMA((beads, n_bead)),
             pltpu.SemaphoreType.DMA((beads, n_bead)),
             pltpu.SemaphoreType.REGULAR((2,)),
+            pltpu.SemaphoreType.DMA((11,)),
         ],
         compiler_params=pltpu.CompilerParams(
-            collective_id=0, has_side_effects=True, vmem_limit_bytes=58 * 1024 * 1024
+            collective_id=0, has_side_effects=True, vmem_limit_bytes=60 * 1024 * 1024
         ),
     )(
         jnp.transpose(coords, (1, 0, 2)),
@@ -514,7 +580,7 @@
         w_out,
         readout.reshape(1, channels),
     )
-    return jnp.transpose(q_next, (1, 0, 2)), jnp.transpose(p_next, (1, 0, 2))
+    return jnp.transpose(result[0], (1, 0, 2)), jnp.transpose(result[1], (1, 0, 2))
 
 
 def solution(mesh):

time: 39 us -> 37.4 us (0.959)
  Pallas kernels: 37.1 us -> 36 us
  local copies, waits for them, and re-layouts: 1.19 us -> 0.6 us
    unnamed x2 -> x0, local copies, waits for them, and re-layouts: 1.19 us -> none
    pallas_call x1, Pallas kernels: 37.1 us -> 36 us  [local(): pl.pallas_call(functools.partial(kernel, n_bead, n_space), out_shape=pltp...]
    transpose x0 -> x1, local copies, waits for them, and re-layouts: none -> 0.6 us  [local(): jnp.transpose(result[1], (1, 0, 2))]
where the time goes in v4:
time: 37.4 us; the launch traced here: 37.3 us
  Pallas kernels  36 us (96%)
  between operations  0.64 us (2%)
  local copies, waits for them, and re-layouts  0.6 us (2%)
    pallas_call x1, Pallas kernels, local(): pl.pallas_call(functools.partial(kernel, n_bead, n_space), out_shape=pltp...  36 us

profile of v4, /device:TPU:32, one launch (start us, length us, event | category | flops | bytes accessed | tf_op | source)
XLA Modules:
  0.0 37.3 jit_solution(323400029765784073)
XLA Ops:
  0.6 36.0 %shard_map.122 = f32[2,3,2,256]{3,2,1,0:T(2,128)S(1)} custom-call(f32[3,2,256]{2,1,0:T(2,128)} %bitcast.14, f32[3,2,256]{2,1,0:T(2,128)} %bitcast.15, s32[1,256]{1,0:T(1,128)} %bitcast.16, f32[256,128]{1,0:T(8,128)} %feats_hbm.1, s32[2,16,256]{2,1,0:T(8,128)} %bitcast.13, s32[2,256]{1,0:T(2,128)} %ghost_rows_hbm.1, f32[5,128]{1,0:T(8,128)} %embed_hbm.1, ...), custom_call_target="tpu_custom_call" | custom-call | tf_op jit(solution)/shard_map/pallas_call | solution.py:505
  36.7 0.6 %slice_bitcast_fusion = (f32[2,3,256]{2,0,1:T(2,128)}, f32[2,3,256]{2,0,1:T(2,128)}) fusion(f32[2,3,2,256]{3,2,1,0:T(2,128)S(1)} %shard_map.122), kind=kLoop, calls=%fused_computation | loop fusion | bytes 24576 | tf_op jit(solution)/shard_map/transpose | solution.py:583

commit v5 on v4

--- a/solution.py
+++ b/solution.py
@@ -301,23 +301,26 @@
 
     def layer_zero(b):
         far = jnp.concatenate([halo0_in[b, 0], halo0_in[b, 1]], axis=1)
+        for g in range(groups):
+            here = chunks[g]
+            got = dot(far, sel[b, atoms:, here])
+            place = got[channels:] + offs[b, :, here]
+            offs[b, 0:8, here] = place[0:8] + place[8:16]
+            gv[b, :, here] = gv[b, :, here] + got[:channels]
+        for here in lanes:
+            off = offs[b, 0:8, here] - pos[b]
+            offs[b, 0:8, here] = off
+            square = jnp.sum(off * off, axis=0, keepdims=True) + SOFTEN
+            inverse = lax.rsqrt(square)
+            offs[b, 8:16, here] = jnp.broadcast_to(inverse, (8, atoms))
+            t = square * inverse - centers
+            apart[b, :, here] = t
+            rads[b, :, here] = stacked(jnp.exp(-WIDTH * (t * t)))
         acc = jnp.zeros((channels, atoms), F32)
         for g in range(groups):
-            got = dot(far, sel[b, atoms:, chunks[g]])
+            weight = dot(wf[0], rads[b, :, chunks[g]])
             for s in range(GROUP):
-                here, there = lanes[g * GROUP + s], lanes[s]
-                place = got[channels:, there] + offs[b, :, here]
-                off = place[0:8] + place[8:16] - pos[b]
-                offs[b, 0:8, here] = off
-                square = jnp.sum(off * off, axis=0, keepdims=True) + SOFTEN
-                inverse = lax.rsqrt(square)
-                offs[b, 8:16, here] = jnp.broadcast_to(inverse, (8, atoms))
-                t = square * inverse - centers
-                apart[b, :, here] = t
-                rads[b, :, here] = stacked(jnp.exp(-WIDTH * (t * t)))
-                value = got[:channels, there] + gv[b, :, here]
-                gv[b, :, here] = value
-                acc = acc + dot(wf[0], rads[b, :, here]) * value
+                acc = acc + weight[:, lanes[s]] * gv[b, :, lanes[g * GROUP + s]]
         update = dot(wo_t[0], acc.astype(BF16))
         u0[b] = update
         hidden = h0[...] + update * jax.nn.sigmoid(update)
@@ -356,22 +359,15 @@
         message = dot(w_out[1], grad.astype(BF16))
         dms[b] = message
         short = message.astype(BF16)
-        total = jnp.zeros((channels, 2 * ghosts), F32)
-        for g in range(groups):
-            for s in range(GROUP):
-                here = lanes[g * GROUP + s]
-                back[b, :, here] = f1_short[b, :, here] * short
-            total = total + dot(back[b, :, chunks[g]], sel_t[b, chunks[g], atoms:])
-        value = total.astype(BF16)
+        for here in lanes:
+            back[b, :, here] = f1_short[b, :, here] * short
+        value = dot(back[b], sel_t[b, :, atoms:]).astype(BF16)
         grad_out[b, 0] = value[:, :ghosts]
         grad_out[b, 1] = value[:, ghosts:]
         start_all(halo(2, b))
 
     def own_scatter(b):
-        total = jnp.zeros((channels, atoms), F32)
-        for g in range(groups):
-            total = total + dot(back[b, :, chunks[g]], sel_t[b, chunks[g], :atoms])
-        dv[b] = total
+        dv[b] = dot(back[b], sel_t[b, :, :atoms])
         for here in lanes:
             t = apart[b, :, here]
             steep = stacked((-2.0 * WIDTH) * (t * jnp.exp(-WIDTH * (t * t))))
@@ -387,22 +383,17 @@
         grad = grad * slope(update, jax.nn.sigmoid(update))
         message = dot(w_out[0], grad.astype(BF16))
         acc = jnp.zeros((8, atoms), F32)
-        total = jnp.zeros((16, 2 * ghosts), F32)
-        for g in range(groups):
-            for s in range(GROUP):
-                here = lanes[g * GROUP + s]
+        for here in lanes:
                 slot = drs[b, :, here] + jnp.sum(message * p0[b, :, here], axis=0, keepdims=True)
                 part = offs[b, 0:8, here] * offs[b, 8:16, here] * slot
                 acc = acc + part
                 parts[b, :, here] = jnp.concatenate(split(part), axis=0)
-            total = total + dot(parts[b, :, chunks[g]], sel_t[b, chunks[g], atoms:])
+        total = dot(parts[b], sel_t[b, :, atoms:])
         total = total[0:8] + total[8:16]
         pgrad_out[b, 0] = total[:, :ghosts]
         pgrad_out[b, 1] = total[:, ghosts:]
         start_all(halo(3, b))
-        total = jnp.zeros((16, atoms), F32)
-        for g in range(groups):
-            total = total + dot(parts[b, :, chunks[g]], sel_t[b, chunks[g], :atoms])
+        total = dot(parts[b], sel_t[b, :, :atoms])
         fown[b] = total[0:8] + total[8:16] - acc
 
     def kick(b):
@@ -454,6 +445,11 @@
     inverse_mass = 1.0 / mass
     arrive(halo(3, 1))
     kick(1)
+    sent = [states()] + [kicks(b) for b in range(beads)]
+    sent += [halo(number, b) for number in range(len(halos)) for b in range(beads)]
+    for copies in sent:
+        for copy in copies:
+            copy.wait_send()
     q_next = [jnp.zeros((4, atoms), F32)] * beads
     p_next = [jnp.zeros((4, atoms), F32)] * beads
     for c in range(beads):
@@ -471,11 +467,6 @@
         for c in range(3):
             out[0, c, b : b + 1, :] = q_base[c, b : b + 1] + q_next[b][c : c + 1, :]
             out[1, c, b : b + 1, :] = p_next[b][c : c + 1, :] - mass * p_base[c, b : b + 1]
-    sent = [states()] + [kicks(b) for b in range(beads)]
-    sent += [halo(number, b) for number in range(len(halos)) for b in range(beads)]
-    for copies in sent:
-        for copy in copies:
-            copy.wait_send()
 
 
 def local(

time: 37.4 us -> 36.2 us (0.968)
  Pallas kernels: 36 us -> 34.9 us
    pallas_call x1, Pallas kernels: 36 us -> 34.9 us  [local(): pl.pallas_call(functools.partial(kernel, n_bead, n_space), out_shape=pltp...]
where the time goes in v5:
time: 36.2 us; the launch traced here: 36.1 us
  Pallas kernels  34.9 us (96%)
  between operations  0.64 us (2%)
  local copies, waits for them, and re-layouts  0.6 us (2%)
    pallas_call x1, Pallas kernels, local(): pl.pallas_call(functools.partial(kernel, n_bead, n_space), out_shape=pltp...  34.9 us

profile of v5, /device:TPU:32, one launch (start us, length us, event | category | flops | bytes accessed | tf_op | source)
XLA Modules:
  0.0 36.1 jit_solution(7004525211617218283)
XLA Ops:
  0.6 34.9 %shard_map.122 = f32[2,3,2,256]{3,2,1,0:T(2,128)S(1)} custom-call(f32[3,2,256]{2,1,0:T(2,128)} %bitcast.14, f32[3,2,256]{2,1,0:T(2,128)} %bitcast.15, s32[1,256]{1,0:T(1,128)} %bitcast.16, f32[256,128]{1,0:T(8,128)} %feats_hbm.1, s32[2,16,256]{2,1,0:T(8,128)} %bitcast.13, s32[2,256]{1,0:T(2,128)} %ghost_rows_hbm.1, f32[5,128]{1,0:T(8,128)} %embed_hbm.1, ...), custom_call_target="tpu_custom_call" | custom-call | tf_op jit(solution)/shard_map/pallas_call | solution.py:496
  35.5 0.6 %slice_bitcast_fusion = (f32[2,3,256]{2,0,1:T(2,128)}, f32[2,3,256]{2,0,1:T(2,128)}) fusion(f32[2,3,2,256]{3,2,1,0:T(2,128)S(1)} %shard_map.122), kind=kLoop, calls=%fused_computation | loop fusion | bytes 24576 | tf_op jit(solution)/shard_map/transpose | solution.py:574

commit v6 on v5

--- a/solution.py
+++ b/solution.py
@@ -322,8 +322,9 @@
             for s in range(GROUP):
                 acc = acc + weight[:, lanes[s]] * gv[b, :, lanes[g * GROUP + s]]
         update = dot(wo_t[0], acc.astype(BF16))
-        u0[b] = update
-        hidden = h0[...] + update * jax.nn.sigmoid(update)
+        gate = jax.nn.sigmoid(update)
+        u0[b] = slope(update, gate)
+        hidden = h0[...] + update * gate
         h1[b] = hidden
         value = dot(wv1_t, hidden.astype(BF16)).astype(BF16)
         v1[b] = value
@@ -379,9 +380,7 @@
         arrived = jnp.concatenate([grad_in[b, 0], grad_in[b, 1]], axis=1)
         value = dv[b] + dot(arrived, given[b])
         grad = dh[b] + dot(w_value[1], value.astype(BF16))
-        update = u0[b]
-        grad = grad * slope(update, jax.nn.sigmoid(update))
-        message = dot(w_out[0], grad.astype(BF16))
+        message = dot(w_out[0], (grad * u0[b]).astype(BF16))
         acc = jnp.zeros((8, atoms), F32)
         for here in lanes:
                 slot = drs[b, :, here] + jnp.sum(message * p0[b, :, here], axis=0, keepdims=True)
@@ -404,10 +403,10 @@
         start_all(kicks(b))
 
     arrive(halo(0, 0))
-    arrive(halo(0, 1))
     pl.semaphore_wait(ready.at[0], len(near))
     signal(ready.at[1], far_out)
     layer_zero(0)
+    arrive(halo(0, 1))
     layer_zero(1)
     between(0)
     pl.semaphore_wait(ready.at[1], len(far_out))
@@ -439,12 +438,12 @@
 
     arrive(halo(3, 0))
     kick(0)
+    arrive(halo(3, 1))
+    kick(1)
     arrive(states())
     q_base = of_positions(keep)
     p_base = of_positions(spring)
     inverse_mass = 1.0 / mass
-    arrive(halo(3, 1))
-    kick(1)
     sent = [states()] + [kicks(b) for b in range(beads)]
     sent += [halo(number, b) for number in range(len(halos)) for b in range(beads)]
     for copies in sent:

time: 36.2 us -> 35.9 us (level)
  Pallas kernels: 34.9 us -> 34.5 us
where the time goes in v6:
time: 35.9 us; the launch traced here: 35.8 us
  Pallas kernels  34.5 us (96%)
  between operations  0.64 us (2%)
  local copies, waits for them, and re-layouts  0.6 us (2%)
    pallas_call x1, Pallas kernels, local(): pl.pallas_call(functools.partial(kernel, n_bead, n_space), out_shape=pltp...  34.5 us

profile of v6, /device:TPU:32, one launch (start us, length us, event | category | flops | bytes accessed | tf_op | source)
XLA Modules:
  0.0 35.8 jit_solution(16877992012482092479)
XLA Ops:
  0.6 34.5 %shard_map.122 = f32[2,3,2,256]{3,2,1,0:T(2,128)S(1)} custom-call(f32[3,2,256]{2,1,0:T(2,128)} %bitcast.14, f32[3,2,256]{2,1,0:T(2,128)} %bitcast.15, s32[1,256]{1,0:T(1,128)} %bitcast.16, f32[256,128]{1,0:T(8,128)} %feats_hbm.1, s32[2,16,256]{2,1,0:T(8,128)} %bitcast.13, s32[2,256]{1,0:T(2,128)} %ghost_rows_hbm.1, f32[5,128]{1,0:T(8,128)} %embed_hbm.1, ...), custom_call_target="tpu_custom_call" | custom-call | tf_op jit(solution)/shard_map/pallas_call | solution.py:495
  35.2 0.6 %slice_bitcast_fusion = (f32[2,3,256]{2,0,1:T(2,128)}, f32[2,3,256]{2,0,1:T(2,128)}) fusion(f32[2,3,2,256]{3,2,1,0:T(2,128)S(1)} %shard_map.122), kind=kLoop, calls=%fused_computation | loop fusion | bytes 24576 | tf_op jit(solution)/shard_map/transpose | solution.py:573

commit v7 on v6

--- a/solution.py
+++ b/solution.py
@@ -392,8 +392,11 @@
         pgrad_out[b, 0] = total[:, :ghosts]
         pgrad_out[b, 1] = total[:, ghosts:]
         start_all(halo(3, b))
+        fown[b] = acc
+
+    def own_positions(b):
         total = dot(parts[b], sel_t[b, :, :atoms])
-        fown[b] = total[0:8] + total[8:16] - acc
+        fown[b] = total[0:8] + total[8:16] - fown[b]
 
     def kick(b):
         arrived = jnp.concatenate([pgrad_in[b, 0], pgrad_in[b, 1]], axis=1)
@@ -422,6 +425,8 @@
     backward(0)
     arrive(halo(2, 1))
     backward(1)
+    own_positions(0)
+    own_positions(1)
 
     keep, drift, spring = ring_tables(beads * n_bead)
 

time: 35.9 us -> 36.2 us (level)
  Pallas kernels: 34.5 us -> 34.9 us
    pallas_call x1, Pallas kernels: 34.5 us -> 34.9 us  [local(): pl.pallas_call(functools.partial(kernel, n_bead, n_space), out_shape=pltp...]
where the time goes in v7:
time: 36.2 us; the launch traced here: 36.1 us
  Pallas kernels  34.9 us (96%)
  between operations  0.64 us (2%)
  local copies, waits for them, and re-layouts  0.6 us (2%)
    pallas_call x1, Pallas kernels, local(): pl.pallas_call(functools.partial(kernel, n_bead, n_space), out_shape=pltp...  34.9 us

profile of v7, /device:TPU:32, one launch (start us, length us, event | category | flops | bytes accessed | tf_op | source)
XLA Modules:
  0.0 36.1 jit_solution(3237235475379039615)
XLA Ops:
  0.6 34.9 %shard_map.122 = f32[2,3,2,256]{3,2,1,0:T(2,128)S(1)} custom-call(f32[3,2,256]{2,1,0:T(2,128)} %bitcast.14, f32[3,2,256]{2,1,0:T(2,128)} %bitcast.15, s32[1,256]{1,0:T(1,128)} %bitcast.16, f32[256,128]{1,0:T(8,128)} %feats_hbm.1, s32[2,16,256]{2,1,0:T(8,128)} %bitcast.13, s32[2,256]{1,0:T(2,128)} %ghost_rows_hbm.1, f32[5,128]{1,0:T(8,128)} %embed_hbm.1, ...), custom_call_target="tpu_custom_call" | custom-call | tf_op jit(solution)/shard_map/pallas_call | solution.py:500
  35.5 0.6 %slice_bitcast_fusion = (f32[2,3,256]{2,0,1:T(2,128)}, f32[2,3,256]{2,0,1:T(2,128)}) fusion(f32[2,3,2,256]{3,2,1,0:T(2,128)S(1)} %shard_map.122), kind=kLoop, calls=%fused_computation | loop fusion | bytes 24576 | tf_op jit(solution)/shard_map/transpose | solution.py:578
